TPU v7x, 256 devices: a whole 4x4x8 slice. The times are simulated.
256 devices in a mesh: seq: 8 (over y, core), exp: 32 (over z, x).
Axes of the slice: x: 4, y: 4, z: 8, core: 2. Of those that a mesh axis runs over, the one named last changes fastest.
Arguments:
- tokens: bfloat16 [32, 4096, 1280], P('exp', 'seq'), may hold values from -64 to 64
- router: bfloat16 [1280, 64], replicated, may hold values from -2 to 2
- w_in: bfloat16 [32, 1280, 5120], P('exp', None, 'seq'), may hold values from -0.15625 to 0.15625
- w_out: bfloat16 [32, 5120, 1280], P('exp', 'seq'), may hold values from -0.078125 to 0.078125
- grad_out: bfloat16 [32, 4096, 1280], P('exp', 'seq'), may hold values from -6 to 6
Outputs:
- mixed: bfloat16 [32, 4096, 1280], P('exp', 'seq')
- d_tokens: bfloat16 [32, 4096, 1280], P('exp', 'seq')
- d_router: float32 [1280, 64], P(('seq', 'exp'))
- d_w_in: bfloat16 [32, 1280, 5120], P('exp', None, 'seq')
- d_w_out: bfloat16 [32, 5120, 1280], P('exp', 'seq')
All inputs are finite; a program needn't handle non-finite values.
Results may differ from a plain program's by a relative error of at most 0.034.
Values may be sent and summed in bfloat16 or wider, within the bound.
A program may use at most 64 MiB of HBM per device.

v0:
```python
import math

import jax
import jax.numpy as jnp
from jax import lax
from jax.sharding import PartitionSpec as P


def gelu_grad(values):
    return 0.5 * (1.0 + lax.erf(values * (1.0 / math.sqrt(2.0)))) + values * jnp.exp(
        -0.5 * values * values
    ) / math.sqrt(2.0 * math.pi)


def to_experts(partial_value):
    summed = lax.psum(partial_value, "seq").astype(jnp.bfloat16)
    return lax.all_to_all(summed, "exp", split_axis=1, concat_axis=0, tiled=True)


def from_experts(partial_value):
    summed = lax.psum(partial_value.astype(jnp.bfloat16), "seq")
    return lax.all_to_all(summed, "exp", split_axis=0, concat_axis=1, tiled=True)


def shards(tokens, router, w_in, w_out, grad_out):
    feats = tokens[0]
    cotangent = grad_out[0]
    width = feats.shape[1]
    logits = lax.dot_general(
        router, feats, (((0,), (1,)), ((), ())), preferred_element_type=jnp.float32
    )
    col_top = lax.pmax(jnp.max(logits, axis=1), "seq")
    col_exp = jnp.exp(logits - col_top[:, None])
    col_total = lax.psum(jnp.sum(col_exp, axis=1), "seq")
    dispatch = col_exp / col_total[:, None]
    dispatch_b = dispatch.astype(jnp.bfloat16)
    partial_in = jnp.dot(dispatch_b, feats, preferred_element_type=jnp.float32)
    row_top = jnp.max(logits, axis=0, keepdims=True)
    row_exp = jnp.exp(logits - row_top)
    combine = row_exp / jnp.sum(row_exp, axis=0, keepdims=True)
    combine_b = combine.astype(jnp.bfloat16)
    rows_in = to_experts(partial_in[None])
    rows = rows_in.reshape(-1, width)
    hidden = jnp.dot(rows, w_in[0], preferred_element_type=jnp.float32)
    activated = jax.nn.gelu(hidden, approximate=False).astype(jnp.bfloat16)
    out_part = jnp.dot(activated, w_out[0], preferred_element_type=jnp.float32)
    slot_output = from_experts(out_part.reshape(rows_in.shape))[0]
    mixed = lax.dot_general(
        combine_b, slot_output, (((0,), (0,)), ((), ())), preferred_element_type=jnp.float32
    ).astype(jnp.bfloat16)
    d_combine = lax.dot_general(
        slot_output, cotangent, (((1,), (1,)), ((), ())), preferred_element_type=jnp.float32
    )
    d_logit_c = combine * (d_combine - jnp.sum(combine * d_combine, axis=0, keepdims=True))
    d_out_part = jnp.dot(combine_b, cotangent, preferred_element_type=jnp.float32)
    d_rows = to_experts(d_out_part[None]).reshape(-1, width)
    d_activated = lax.dot_general(
        d_rows, w_out[0], (((1,), (1,)), ((), ())), preferred_element_type=jnp.float32
    )
    d_hidden = (d_activated * gelu_grad(hidden)).astype(jnp.bfloat16)
    d_w_out = lax.dot_general(
        activated, d_rows, (((0,), (0,)), ((), ())), preferred_element_type=jnp.float32
    )
    d_w_in = lax.dot_general(
        rows, d_hidden, (((0,), (0,)), ((), ())), preferred_element_type=jnp.float32
    )
    d_in_part = lax.dot_general(
        d_hidden, w_in[0], (((1,), (1,)), ((), ())), preferred_element_type=jnp.float32
    )
    slot_input_gradient = from_experts(d_in_part.reshape(rows_in.shape))[0]
    d_dispatch = lax.dot_general(
        slot_input_gradient, feats, (((1,), (1,)), ((), ())), preferred_element_type=jnp.float32
    )
    column_sum = lax.psum(jnp.sum(dispatch * d_dispatch, axis=1), "seq")
    d_logit_d = dispatch * (d_dispatch - column_sum[:, None])
    d_logit_b = (d_logit_c + d_logit_d).astype(jnp.bfloat16)
    d_feats = lax.dot_general(
        dispatch_b,
        slot_input_gradient,
        (((0,), (0,)), ((), ())),
        preferred_element_type=jnp.float32,
    )
    d_feats = d_feats + lax.dot_general(
        d_logit_b, router, (((0,), (1,)), ((), ())), preferred_element_type=jnp.float32
    )
    d_router = lax.psum_scatter(
        lax.dot_general(
            feats, d_logit_b, (((0,), (1,)), ((), ())), preferred_element_type=jnp.float32
        ),
        ("seq", "exp"),
        scatter_dimension=0,
        tiled=True,
    )
    return (
        mixed[None],
        d_feats.astype(jnp.bfloat16)[None],
        d_router,
        d_w_in.astype(jnp.bfloat16)[None],
        d_w_out.astype(jnp.bfloat16)[None],
    )


def solution(mesh):
    in_specs = (
        P("exp", "seq", None),
        P(),
        P("exp", None, "seq"),
        P("exp", "seq", None),
        P("exp", "seq", None),
    )
    out_specs = (
        P("exp", "seq", None),
        P("exp", "seq", None),
        P(("seq", "exp"), None),
        P("exp", None, "seq"),
        P("exp", "seq", None),
    )
    return jax.shard_map(shards, mesh=mesh, in_specs=in_specs, out_specs=out_specs, check_vma=False)
```

profile of v0, /device:TPU:1, one launch (start us, length us, event | category | flops | bytes accessed | tf_op | source)
XLA Modules:
  0.0 486.9 jit_solution(15661714093425016987)
XLA Ops:
  7.2 2.2 fusion.63
  9.4 15.0 %pmax.7 = f32[64]{0:T(128)S(1)} all-reduce(f32[64]{0:T(128)S(1)} %get-tuple-element.30), channel_id=1, replica_groups=mesh['seq'=8,'exp'=32] {'seq'}, use_global_device_ids=true, to_apply=%region_3.0 | all-reduce | flops 64 | bytes 512 | tf_op jit(solution)/shard_map/pmax | solution.py:32
  26.2 13.1 %psum.42 = f32[64]{0:T(128)S(1)} all-reduce(f32[64]{0:T(128)S(1)} %get-tuple-element.28), channel_id=1, replica_groups=mesh['seq'=8,'exp'=32] {'seq'}, use_global_device_ids=true, to_apply=%region_5.0 | all-reduce | flops 64 | bytes 512 | tf_op jit(solution)/shard_map/psum | solution.py:34
  40.5 27.4 %all-reduce.10 = (bf16[1,64,1280]{2,1,0:T(8,128)(2,1)}, bf16[1,64,1280]{2,1,0:T(8,128)(2,1)}) all-reduce(f32[1,64,1280]{2,1,0:T(8,128)} %convolution_bitcast_fusion.2, f32[1,64,1280]{2,1,0:T(8,128)S(1)} %convolution_bitcast_fusion.1), channel_id=1, replica_groups=mesh['seq'=8,'exp'=32] {'seq'}, use_global_device_ids=true, to_apply=%region_6.0 | all-reduce | flops 163840 | bytes 983040 | tf_op jit(solution)/shard_map/psum | solution.py:16
  69.6 2.3 reduce
  73.5 11.1 %all-to-all-start = ((bf16[32,2,1280]{2,1,0:T(2,128)(2,1)}), bf16[32,2,1280]{2,1,0:T(2,128)(2,1)}, u32[]{:S(2)}, u32[]{:S(2)}) async-start(bf16[32,2,1280]{2,1,0:T(2,128)(2,1)} %reshape.48), calls=%async_computation | async-start | bytes 327680 | tf_op jit(solution)/shard_map/all_to_all | solution.py:17
  85.8 2.3 reduce.1
  89.7 4.5 all-to-all-done
  94.2 4.7 all-to-all-start.2
  101.9 6.7 %all-to-all-done.2 = bf16[32,2,1280]{2,1,0:T(2,128)(2,1)} async-done(((bf16[32,2,1280]{2,1,0:T(2,128)(2,1)}), bf16[32,2,1280]{2,1,0:T(2,128)(2,1)}, u32[]{:S(2)}, u32[]{:S(2)}) %all-to-all-start.2) | async-done | bytes 163872 | tf_op jit(solution)/shard_map/all_to_all | solution.py:17
  110.0 2.1 fusion.23
  112.8 2.2 convolution_convert_fusion.3
  116.5 2.5 convolution_convert_fusion.4
  119.0 61.8 %all-reduce.9.cloned.1.call-done = (bf16[32,2,1280]{2,0,1:T(8,128)(2,1)}, bf16[32,2,1280]{2,0,1:T(8,128)(2,1)}) async-done(((bf16[32,2,1280]{2,0,1:T(8,128)(2,1)}, bf16[32,2,1280]{2,0,1:T(8,128)(2,1)}), (bf16[32,2,1280]{2,0,1:T(8,128)(2,1)}, bf16[32,2,1280]{2,0,1:T(8,128)(2,1)})) %all-reduce.9.cloned.1.call-update) | async-done | bytes 327696 | tf_op jit(solution)/shard_map/psum | solution.py:21
  182.6 9.6 %all-to-all-start.3 = ((bf16[32,2,1280]{2,1,0:T(2,128)(2,1)}), bf16[32,2,1280]{2,1,0:T(2,128)(2,1)}, u32[]{:S(2)}, u32[]{:S(2)}) async-start(bf16[32,2,1280]{2,1,0:T(2,128)(2,1)} %copy.30), calls=%async_computation.3 | async-start | bytes 327680 | tf_op jit(solution)/shard_map/all_to_all | solution.py:22
  192.3 2.8 fusion.1
  197.7 4.2 all-to-all-done.3
  201.9 5.1 %all-to-all-start.1 = ((bf16[32,2,1280]{2,1,0:T(2,128)(2,1)}), bf16[32,2,1280]{2,1,0:T(2,128)(2,1)}, u32[]{:S(2)}, u32[]{:S(2)}) async-start(bf16[32,2,1280]{2,1,0:T(2,128)(2,1)} %copy.27), calls=%async_computation.1 | async-start | bytes 327680 | tf_op jit(solution)/shard_map/all_to_all | solution.py:22
  208.6 2.1 fusion.54
  210.7 5.9 %all-to-all-done.1 = bf16[32,2,1280]{2,1,0:T(2,128)(2,1)} async-done(((bf16[32,2,1280]{2,1,0:T(2,128)(2,1)}), bf16[32,2,1280]{2,1,0:T(2,128)(2,1)}, u32[]{:S(2)}, u32[]{:S(2)}) %all-to-all-start.1) | async-done | bytes 163872 | tf_op jit(solution)/shard_map/all_to_all | solution.py:22
  217.6 3.1 multiply_reduce_fusion.1
  220.7 17.1 %psum.47 = f32[64]{0:T(128)} all-reduce(f32[64]{0:T(128)} %get-tuple-element.26), channel_id=1, replica_groups=mesh['seq'=8,'exp'=32] {'seq'}, use_global_device_ids=true, to_apply=%region_12.0 | all-reduce | flops 64 | bytes 512 | tf_op jit(solution)/shard_map/psum | solution.py:74
  239.9 3.5 fusion.4
  245.0 233.5 %all-reduce.7.cloned.1.call-done = f32[1280,64]{0,1:T(8,128)} async-done(((f32[1280,64]{0,1:T(8,128)}), f32[1280,64]{0,1:T(8,128)}) %all-reduce.7.cloned.1.call-update) | async-done | bytes 327696
  (39 shorter events, 27.8 us)
Async XLA Ops:
  7.2 93.3 %copy-start = (bf16[1,1280,640]{2,1,0:T(8,128)(2,1)S(1)}, bf16[1,1280,640]{2,1,0:T(8,128)(2,1)}, u32[]{:S(2)}) copy-start(bf16[1,1280,640]{2,1,0:T(8,128)(2,1)} %param.7) | copy-start | bytes 4915204
  7.2 32.2 %copy-start.1 = (bf16[1,512,1280]{2,1,0:T(8,128)(2,1)S(1)}, bf16[1,512,1280]{2,1,0:T(8,128)(2,1)}, u32[]{:S(2)}) copy-start(bf16[1,512,1280]{2,1,0:T(8,128)(2,1)} %param.5) | copy-start | bytes 3932164
  73.5 20.8 %all-to-all-start = ((bf16[32,2,1280]{2,1,0:T(2,128)(2,1)}), bf16[32,2,1280]{2,1,0:T(2,128)(2,1)}, u32[]{:S(2)}, u32[]{:S(2)}) async-start(bf16[32,2,1280]{2,1,0:T(2,128)(2,1)} %reshape.48), calls=%async_computation | async-start | bytes 327680 | tf_op jit(solution)/shard_map/all_to_all | solution.py:17
  94.2 14.4 %all-to-all-start.2 = ((bf16[32,2,1280]{2,1,0:T(2,128)(2,1)}), bf16[32,2,1280]{2,1,0:T(2,128)(2,1)}, u32[]{:S(2)}, u32[]{:S(2)}) async-start(bf16[32,2,1280]{2,1,0:T(2,128)(2,1)} %reshape.50), calls=%async_computation.2 | async-start | bytes 327680 | tf_op jit(solution)/shard_map/all_to_all | solution.py:17
  99.0 81.9 %all-reduce.9.cloned.1.call-start = ((), (), s32[]{:S(2)}) async-start(), calls=%async_computation.5 | async-start | bytes 655360 | tf_op jit(solution)/shard_map/psum | solution.py:21
  100.5 1.4 copy-start.2
  182.6 19.3 %all-to-all-start.3 = ((bf16[32,2,1280]{2,1,0:T(2,128)(2,1)}), bf16[32,2,1280]{2,1,0:T(2,128)(2,1)}, u32[]{:S(2)}, u32[]{:S(2)}) async-start(bf16[32,2,1280]{2,1,0:T(2,128)(2,1)} %copy.30), calls=%async_computation.3 | async-start | bytes 327680 | tf_op jit(solution)/shard_map/all_to_all | solution.py:22
  192.3 2.8 copy-start.4
  192.3 4.6 copy-start.5
  201.9 14.7 %all-to-all-start.1 = ((bf16[32,2,1280]{2,1,0:T(2,128)(2,1)}), bf16[32,2,1280]{2,1,0:T(2,128)(2,1)}, u32[]{:S(2)}, u32[]{:S(2)}) async-start(bf16[32,2,1280]{2,1,0:T(2,128)(2,1)} %copy.27), calls=%async_computation.1 | async-start | bytes 327680 | tf_op jit(solution)/shard_map/all_to_all | solution.py:22
  207.0 271.5 %all-reduce.7.cloned.1.call-start = ((), (), s32[]{:S(2)}) async-start(), calls=%async_computation.4 | async-start | bytes 655360
  220.7 19.2 %copy-start.3 = (bf16[1280,64]{0,1:T(8,128)(2,1)S(1)}, bf16[1280,64]{0,1:T(8,128)(2,1)}, u32[]{:S(2)}) copy-start(bf16[1280,64]{0,1:T(8,128)(2,1)} %param.6) | copy-start | bytes 491524
Sparse Core Ops, SparseCore 0:
  119.1 61.6 all-reduce.8
  240.0 238.4 all-reduce.6
where the time goes:
time: 488 us; the launch traced here: 487 us
  waiting for transfers between devices  317 us (65%)
  blocking collectives  72.6 us (15%)
  starting transfers between devices  30.7 us (6%)
  matrix products  30.5 us (6%)
  local copies, waits for them, and re-layouts  17.4 us (4%)
  between operations  14.2 us (3%)
    unnamed x3, waiting for transfers between devices  234 us
    psum x1, waiting for transfers between devices, from_experts(): summed = lax.psum(partial_value.astype(jnp.bfloat16), 'seq')  61.8 us
    psum x1, blocking collectives, to_experts(): summed = lax.psum(partial_value, 'seq').astype(jnp.bfloat16)  27.4 us
    psum x1, blocking collectives, shards(): column_sum = lax.psum(jnp.sum(dispatch * d_dispatch, axis=1), 'seq')  17.1 us
    all_to_all x2, starting transfers between devices, to_experts(): lax.all_to_all(summed, 'exp', split_axis=1, concat_axis=0, tiled=True)  15.9 us
    pmax x1, blocking collectives, shards(): col_top = lax.pmax(jnp.max(logits, axis=1), 'seq')  15 us
    all_to_all x2, starting transfers between devices, from_experts(): lax.all_to_all(summed, 'exp', split_axis=0, concat_axis=1, tiled=True)  14.7 us
    psum x1, blocking collectives, shards(): col_total = lax.psum(jnp.sum(col_exp, axis=1), 'seq')  13.1 us
  transfers between devices with their start and end apart: 6, of which 6 were waited for; matrix products, arithmetic and copies ran while one was open for 5% of the time, Pallas kernels for 0%

commit v1 on v0

v1 whole, which is shorter than its diff:
```python
import math

import jax
import jax.numpy as jnp
from jax import lax
from jax.experimental import pallas as pl
from jax.experimental.pallas import tpu as pltpu
from jax.sharding import PartitionSpec as P

F32 = jnp.float32
BF16 = jnp.bfloat16
MESH = pl.DeviceIdType.MESH
SEQ = 8
EXP = 32
XS = 4
D = 1280
H = 640
T = 512
S = 64


def nn(a, b):
    return lax.dot_general(a, b, (((1,), (0,)), ((), ())), preferred_element_type=F32)


def nt(a, b):
    return lax.dot_general(a, b, (((1,), (1,)), ((), ())), preferred_element_type=F32)


def fold(a):
    lo = a[:, :H].reshape(SEQ, 8, H)
    hi = a[:, H:].reshape(SEQ, 8, H)
    return jnp.concatenate([lo, hi], axis=1).astype(BF16)


def unfold(a):
    a = a.astype(F32)
    lo = a[:, :8].reshape(S, H)
    hi = a[:, 8:].reshape(S, H)
    return jnp.concatenate([lo, hi], axis=1).astype(BF16)


def column_to_rows(top, low):
    square = jnp.concatenate(
        [jnp.broadcast_to(top, (S, 128)), jnp.broadcast_to(low, (S, 128))], axis=0
    )
    return square.T[:8]


def rows_to_column(rows):
    return jnp.concatenate([rows] * 16, axis=0).T


def kernel(
    tokens_hbm, router_hbm, w_in_hbm, w_out_hbm, grad_hbm,
    mixed_hbm, d_tokens_hbm, d_router_hbm, d_w_in_hbm, d_w_out_hbm,
    tok, rout, w_in, w_out, grad, mixed_v, d_tok_v, d_rout_v, d_w_in_v, d_w_out_v,
    rs_send, rs_recv, ex_send, ex_recv, ag, stat_send, stat_recv, col_send, col_recv,
    r1_send, r1_recv, r1_sum, r2_send, r2_recv,
    in_sem, out_sem, rs_ss, rs_rs, ex_ss, ex_rs, ag_ss, ag_rs, st_ss, st_rs, r_ss, r_rs,
):
    me_s = lax.axis_index("seq")
    me_n = lax.axis_index("exp")
    z = me_n // XS
    x = lax.rem(me_n, XS)
    partner = lax.rem(me_s - z + SEQ, SEQ)

    loads = [
        pltpu.make_async_copy(src, dst, in_sem.at[i])
        for i, (src, dst) in enumerate(
            ((router_hbm, rout), (tokens_hbm, tok), (grad_hbm, grad), (w_out_hbm, w_out), (w_in_hbm, w_in))
        )
    ]
    for load in loads:
        load.start()

    barrier = pltpu.get_barrier_semaphore()

    def greet_seq(k, carry):
        pl.semaphore_signal(
            barrier, inc=1, device_id=(lax.rem(me_s + k, SEQ), me_n), device_id_type=MESH
        )
        return carry

    def greet_exp(k, carry):
        pl.semaphore_signal(
            barrier, inc=1, device_id=(me_s, lax.rem(me_n + k, EXP)), device_id_type=MESH
        )
        return carry

    lax.fori_loop(1, SEQ, greet_seq, 0)
    lax.fori_loop(1, EXP, greet_exp, 0)

    def over_seq(make):
        def step(k, carry):
            make(lax.rem(me_s + k, SEQ)).start()
            return carry

        lax.fori_loop(1, SEQ, step, 0)

    def all_of(ref, sem):
        pltpu.make_async_copy(ref, ref, sem).wait()

    def rs_start(i):
        rs_recv[i, me_s] = rs_send[i, partner]
        over_seq(
            lambda p: pltpu.make_async_remote_copy(
                src_ref=rs_send.at[i, lax.rem(p - z + SEQ, SEQ)],
                dst_ref=rs_recv.at[i, me_s],
                send_sem=rs_ss.at[i], recv_sem=rs_rs.at[i],
                device_id=(p, me_n), device_id_type=MESH,
            )
        )

    def rs_finish_ex_start(i):
        all_of(rs_recv.at[i, pl.ds(0, SEQ - 1)], rs_rs.at[i])
        total = rs_recv[i, 0].astype(F32)
        for k in range(1, SEQ):
            total = total + rs_recv[i, k].astype(F32)
        rows = jnp.concatenate([total[:8], total[8:]], axis=1)
        for k in range(XS):
            ex_send[i, k] = rows[2 * k : 2 * k + 2]
        for k in range(XS):
            to = XS * partner + k

            @pl.when(to != me_n)
            def _():
                pltpu.make_async_remote_copy(
                    src_ref=ex_send.at[i, k], dst_ref=ex_recv.at[i, x],
                    send_sem=ex_ss.at[i], recv_sem=ex_rs.at[i],
                    device_id=(me_s, to), device_id_type=MESH,
                ).start()

            @pl.when(to == me_n)
            def _():
                ex_recv[i, x] = ex_send[i, k]

    def ex_finish_ag_start(i):
        @pl.when(partner != z)
        def _():
            all_of(ex_recv.at[i], ex_rs.at[i])

        @pl.when(partner == z)
        def _():
            all_of(ex_recv.at[i, pl.ds(0, XS - 1)], ex_rs.at[i])

        rows = jnp.concatenate([ex_recv[i, k] for k in range(XS)], axis=0)
        ag[i, partner] = jnp.concatenate([rows[:, :H], rows[:, H:]], axis=0).astype(BF16)
        over_seq(
            lambda p: pltpu.make_async_remote_copy(
                src_ref=ag.at[i, partner], dst_ref=ag.at[i, partner],
                send_sem=ag_ss.at[i], recv_sem=ag_rs.at[i],
                device_id=(p, me_n), device_id_type=MESH,
            )
        )

    def ag_finish(i):
        all_of(ag.at[i, pl.ds(0, SEQ - 1)], ag_rs.at[i])
        return unfold(ag[i])

    def stat_start(i, send, recv):
        recv[me_s] = send[...]
        over_seq(
            lambda p: pltpu.make_async_remote_copy(
                src_ref=send, dst_ref=recv.at[me_s],
                send_sem=st_ss.at[i], recv_sem=st_rs.at[i],
                device_id=(p, me_n), device_id_type=MESH,
            )
        )

    loads[0].wait()
    router_t = rout[...].astype(F32).T.astype(BF16)
    loads[1].wait()
    logits = nt(router_t, tok[...])
    own_top = jnp.max(logits, axis=1, keepdims=True)
    own_exp = jnp.exp(logits - own_top)
    own_total = jnp.sum(own_exp, axis=1, keepdims=True)
    stat_send[...] = column_to_rows(own_top, own_total)
    pl.semaphore_wait(barrier, SEQ - 1 + EXP - 1)
    stat_start(0, stat_send, stat_recv)
    row_exp = jnp.exp(logits - jnp.max(logits, axis=0, keepdims=True))
    combine = row_exp / jnp.sum(row_exp, axis=0, keepdims=True)

    loads[2].wait()
    rs_send[0] = fold(nn(combine.astype(BF16), grad[...]))
    rs_start(0)
    in_part = nn(own_exp.astype(BF16), tok[...])
    all_of(stat_recv.at[pl.ds(0, SEQ - 1)], st_rs.at[0])
    stats = [stat_recv[k] for k in range(SEQ)]
    top = stats[0]
    for k in range(1, SEQ):
        top = jnp.maximum(top, stats[k])
    lane = lax.broadcasted_iota(jnp.int32, (8, 128), 1)
    top = jnp.where(lane < S, top, 0.0)
    total = jnp.zeros((8, 128), F32)
    for k in range(SEQ):
        shift = jnp.where(lane < S, stats[k] - top, 0.0)
        total = total + pltpu.roll(stats[k], S, 1) * jnp.exp(shift)
    merged = rows_to_column(jnp.where(lane < S, top, pltpu.roll(total, S, 1)))
    scale = jnp.exp(own_top - merged[:S, :1]) / merged[S:, :1]
    rs_send[1] = fold(in_part * scale)
    rs_start(1)
    dispatch = own_exp * scale

    rs_finish_ex_start(0)
    rs_finish_ex_start(1)
    ex_finish_ag_start(0)
    ex_finish_ag_start(1)

    loads[3].wait()
    d_rows = ag_finish(0)
    d_act = nt(d_rows, w_out[...])
    loads[4].wait()
    rows = ag_finish(1)
    hidden = nn(rows, w_in[...])
    cdf = 0.5 * (1.0 + lax.erf(hidden * (1.0 / math.sqrt(2.0))))
    act = hidden * cdf
    pdf = jnp.exp(-0.5 * hidden * hidden) * (1.0 / math.sqrt(2.0 * math.pi))
    d_hidden = d_act * (cdf + hidden * pdf)
    d_hidden_b = d_hidden.astype(BF16)
    rs_send[2] = fold(nt(d_hidden_b, w_in[...]))
    rs_start(2)
    rs_send[3] = fold(nn(act.astype(BF16), w_out[...]))
    rs_start(3)

    rs_finish_ex_start(2)
    rs_finish_ex_start(3)
    act_t = act.T.astype(BF16)
    for k in range(5):
        part = slice(128 * k, 128 * k + 128)
        d_w_out_v[part] = nn(act_t[part], d_rows).astype(BF16)
    out0 = pltpu.make_async_copy(d_w_out_v, d_w_out_hbm, out_sem.at[0])
    out0.start()
    ex_finish_ag_start(2)
    ex_finish_ag_start(3)
    rows_t = rows.astype(F32).T.astype(BF16)
    for k in range(10):
        part = slice(128 * k, 128 * k + 128)
        d_w_in_v[part] = nn(rows_t[part], d_hidden_b).astype(BF16)
    out1 = pltpu.make_async_copy(d_w_in_v, d_w_in_hbm, out_sem.at[1])
    out1.start()

    d_slots = ag_finish(2)
    d_dispatch = nt(d_slots, tok[...])
    weighted = dispatch * d_dispatch
    column = jnp.sum(weighted, axis=1, keepdims=True)
    col_send[...] = column_to_rows(column, column)
    stat_start(1, col_send, col_recv)
    slots_out = ag_finish(3)
    d_combine = nt(slots_out, grad[...])
    d_logit_c = combine * (d_combine - jnp.sum(combine * d_combine, axis=0, keepdims=True))
    combine_t = combine.T.astype(BF16)
    for k in range(4):
        part = slice(128 * k, 128 * k + 128)
        mixed_v[part] = nn(combine_t[part], slots_out).astype(BF16)
    out2 = pltpu.make_async_copy(mixed_v, mixed_hbm, out_sem.at[2])
    out2.start()
    all_of(col_recv.at[pl.ds(0, SEQ - 1)], st_rs.at[1])
    total = col_recv[0]
    for k in range(1, SEQ):
        total = total + col_recv[k]
    column_sum = rows_to_column(total)[:S, :1]
    d_logit = d_logit_c + dispatch * (d_dispatch - column_sum)

    d_router_t = nn(d_logit.astype(BF16), tok[...])
    pair = jnp.concatenate([d_router_t, pltpu.roll(d_router_t, D - 80, 1)], axis=0).T
    for k in range(SEQ):
        r1_send[k] = pair[160 * k : 160 * k + 80]
    r1_recv[me_s] = r1_send[me_s]
    over_seq(
        lambda p: pltpu.make_async_remote_copy(
            src_ref=r1_send.at[p], dst_ref=r1_recv.at[me_s],
            send_sem=r_ss.at[0], recv_sem=r_rs.at[0],
            device_id=(p, me_n), device_id_type=MESH,
        )
    )
    weights = jnp.concatenate([dispatch, d_logit], axis=0).T.astype(BF16)
    values = jnp.concatenate([d_slots, router_t], axis=0)
    for k in range(4):
        part = slice(128 * k, 128 * k + 128)
        d_tok_v[part] = nn(weights[part], values).astype(BF16)
    out3 = pltpu.make_async_copy(d_tok_v, d_tokens_hbm, out_sem.at[3])
    out3.start()
    all_of(r1_recv.at[pl.ds(0, SEQ - 1)], r_rs.at[0])
    total = r1_recv[0]
    for k in range(1, SEQ):
        total = total + r1_recv[k]
    r1_sum[0:80] = total
    r1_sum[80:88] = jnp.zeros((8, 128), F32)
    for k in range(16):
        r2_send[k] = r1_sum[5 * k : 5 * k + 8]
    r2_recv[me_n] = r2_send[lax.rem(me_n, 16)]

    def final(k, carry):
        to = lax.rem(me_n + k, EXP)
        pltpu.make_async_remote_copy(
            src_ref=r2_send.at[lax.rem(to, 16)], dst_ref=r2_recv.at[me_n],
            send_sem=r_ss.at[1], recv_sem=r_rs.at[1],
            device_id=(me_s, to), device_id_type=MESH,
        ).start()
        return carry

    lax.fori_loop(1, EXP, final, 0)
    all_of(r2_recv.at[pl.ds(0, EXP - 1)], r_rs.at[1])
    total = r2_recv[0]
    for k in range(1, EXP):
        total = total + r2_recv[k]
    high = me_n >= 16
    total = jnp.where(high, pltpu.roll(total, S, 1), total)
    d_rout_v[...] = total[:5, :S]
    out4 = pltpu.make_async_copy(d_rout_v, d_router_hbm, out_sem.at[4])
    out4.start()

    for i in range(4):
        all_of(rs_send.at[i, pl.ds(0, SEQ - 1)], rs_ss.at[i])

        @pl.when(partner != z)
        def _():
            all_of(ex_send.at[i], ex_ss.at[i])

        @pl.when(partner == z)
        def _():
            all_of(ex_send.at[i, pl.ds(0, XS - 1)], ex_ss.at[i])

        all_of(ag.at[i, pl.ds(0, SEQ - 1)], ag_ss.at[i])
    all_of(stat_recv.at[pl.ds(0, SEQ - 1)], st_ss.at[0])
    all_of(col_recv.at[pl.ds(0, SEQ - 1)], st_ss.at[1])
    all_of(r1_send.at[pl.ds(0, SEQ - 1)], r_ss.at[0])
    all_of(r2_recv.at[pl.ds(0, EXP - 1)], r_ss.at[1])
    for out in (out0, out1, out2, out3, out4):
        out.wait()


def shards(tokens, router, w_in, w_out, grad_out):
    any_space = pl.BlockSpec(memory_space=pl.ANY)
    dma = pltpu.SemaphoreType.DMA
    mixed, d_tokens, d_router, d_w_in, d_w_out = pl.pallas_call(
        kernel,
        out_shape=(
            jax.ShapeDtypeStruct((T, D), BF16),
            jax.ShapeDtypeStruct((T, D), BF16),
            jax.ShapeDtypeStruct((5, S), F32),
            jax.ShapeDtypeStruct((D, H), BF16),
            jax.ShapeDtypeStruct((H, D), BF16),
        ),
        in_specs=[any_space] * 5,
        out_specs=[any_space] * 5,
        scratch_shapes=[
            pltpu.VMEM((T, D), BF16),
            pltpu.VMEM((D, S), BF16),
            pltpu.VMEM((D, H), BF16),
            pltpu.VMEM((H, D), BF16),
            pltpu.VMEM((T, D), BF16),
            pltpu.VMEM((T, D), BF16),
            pltpu.VMEM((T, D), BF16),
            pltpu.VMEM((5, S), F32),
            pltpu.VMEM((D, H), BF16),
            pltpu.VMEM((H, D), BF16),
            pltpu.VMEM((4, SEQ, 16, H), BF16),
            pltpu.VMEM((4, SEQ, 16, H), BF16),
            pltpu.VMEM((4, XS, 2, D), F32),
            pltpu.VMEM((4, XS, 2, D), F32),
            pltpu.VMEM((4, SEQ, 16, H), BF16),
            pltpu.VMEM((8, 128), F32),
            pltpu.VMEM((SEQ, 8, 128), F32),
            pltpu.VMEM((8, 128), F32),
            pltpu.VMEM((SEQ, 8, 128), F32),
            pltpu.VMEM((SEQ, 80, 128), F32),
            pltpu.VMEM((SEQ, 80, 128), F32),
            pltpu.VMEM((88, 128), F32),
            pltpu.VMEM((16, 8, 128), F32),
            pltpu.VMEM((EXP, 8, 128), F32),
            dma((5,)), dma((5,)), dma((4,)), dma((4,)), dma((4,)), dma((4,)), dma((4,)), dma((4,)),
            dma((2,)), dma((2,)), dma((2,)), dma((2,)),
        ],
        compiler_params=pltpu.CompilerParams(
            collective_id=0, has_side_effects=True, vmem_limit_bytes=48 * 1024 * 1024
        ),
    )(tokens[0], router, w_in[0], w_out[0], grad_out[0])
    return mixed[None], d_tokens[None], d_router, d_w_in[None], d_w_out[None]


def solution(mesh):
    in_specs = (
        P("exp", "seq", None),
        P(),
        P("exp", None, "seq"),
        P("exp", "seq", None),
        P("exp", "seq", None),
    )
    out_specs = (
        P("exp", "seq", None),
        P("exp", "seq", None),
        P(("seq", "exp"), None),
        P("exp", None, "seq"),
        P("exp", "seq", None),
    )
    return jax.shard_map(shards, mesh=mesh, in_specs=in_specs, out_specs=out_specs, check_vma=False)
```

time: 488 us -> 74.6 us (0.15)
  waiting for transfers between devices: 317 us -> 0 us
  blocking collectives: 72.6 us -> 0 us
  Pallas kernels: 0 us -> 63.8 us
  starting transfers between devices: 30.7 us -> 0 us
  matrix products: 30.5 us -> 0 us
  between operations: 14.2 us -> 0.66 us
  local copies, waits for them, and re-layouts: 17.4 us -> 9.91 us
    unnamed x3 -> x0, waiting for transfers between devices: 234 us -> none
    pallas_call x0 -> x1, Pallas kernels: none -> 63.8 us  [shards(): pl.pallas_call(kernel, out_shape=(jax.ShapeDtypeStruct((T, D), BF16), jax...]
    psum x1 -> x0, waiting for transfers between devices: 61.8 us -> none  [from_experts(): summed = lax.psum(partial_value.astype(jnp.bfloat16), 'seq')]
    psum x3 -> x0, blocking collectives: 57.6 us -> none  [the longest x1 27.4 us: to_experts(): summed = lax.psum(partial_value, 'seq').astype(jnp.bfloat16)]
    all_to_all x4 -> x0, starting transfers between devices: 30.6 us -> none  [the longest x2 15.9 us: to_experts(): lax.all_to_all(summed, 'exp', split_axis=1, concat_axis=0, tiled=True)]
    dot_general x15 -> x0, matrix products: 30.5 us -> none  [the longest x1 3.52 us: shards(): lax.dot_general(d_logit_b, router, (((0,), (1,)), ((), ())), preferred_el...]
    all_to_all x4 -> x0, waiting for transfers between devices: 21.4 us -> none  [the longest x2 11.2 us: to_experts(): lax.all_to_all(summed, 'exp', split_axis=1, concat_axis=0, tiled=True)]
    pmax x1 -> x0, blocking collectives: 15 us -> none  [shards(): col_top = lax.pmax(jnp.max(logits, axis=1), 'seq')]
  transfers between devices with their start and end apart: 6 -> 0, of which waited for: 6 -> 0; matrix products, arithmetic and copies ran while one was open for 5% -> 0% of each run, Pallas kernels for 0% -> 0%
where the time goes in v1:
time: 74.6 us; the launch traced here: 74.4 us
  Pallas kernels  63.8 us (86%)
  local copies, waits for them, and re-layouts  9.91 us (13%)
    pallas_call x1, Pallas kernels, shards(): pl.pallas_call(kernel, out_shape=(jax.ShapeDtypeStruct((T, D), BF16), jax...  63.8 us
    unnamed x14, local copies, waits for them, and re-layouts  9.91 us

profile of v1, /device:TPU:1, one launch (start us, length us, event | category | flops | bytes accessed | tf_op | source)
XLA Modules:
  0.0 74.4 jit_solution(12501188260245467921)
XLA Ops:
  0.6 1.1 %copy.10.router_hbm = bf16[1280,64]{1,0:T(8,128)(2,1)S(1)} copy(bf16[1280,64]{0,1:T(8,128)(2,1)} %param.6) | data formatting | bytes 327680 | tf_op args[1]
  1.8 0.0 copy-start
  1.8 1.3 %copy-done = bf16[1,512,1280]{2,1,0:T(8,128)(2,1)S(1)} copy-done((bf16[1,512,1280]{2,1,0:T(8,128)(2,1)S(1)}, bf16[1,512,1280]{2,1,0:T(8,128)(2,1)}, u32[]{:S(2)}) %copy-start) | copy-done | bytes 1310744
  3.1 0.0 copy-start.1
  3.1 1.3 %copy-done.1 = bf16[1,512,1280]{2,1,0:T(8,128)(2,1)S(1)} copy-done((bf16[1,512,1280]{2,1,0:T(8,128)(2,1)S(1)}, bf16[1,512,1280]{2,1,0:T(8,128)(2,1)}, u32[]{:S(2)}) %copy-start.1) | copy-done | bytes 1310744
  4.4 63.8 %shard_map.92 = (bf16[512,1280]{1,0:T(8,128)(2,1)S(1)}, bf16[512,1280]{1,0:T(8,128)(2,1)S(1)}, f32[5,64]{1,0:T(8,128)S(1)}, bf16[1280,640]{1,0:T(8,128)(2,1)}, bf16[640,1280]{1,0:T(8,128)(2,1)}) custom-call(bf16[512,1280]{1,0:T(8,128)(2,1)S(1)} %bitcast.10, bf16[1280,64]{1,0:T(8,128)(2,1)S(1)} %copy.10.router_hbm, bf16[1280,640]{1,0:T(8,128)(2,1)} %bitcast.12, ...), custom_call_target="tpu_custom_call" | custom-call | tf_op jit(solution)/shard_map/pallas_call | solution.py:337
  68.3 1.1 %copy.16 = bf16[1,512,1280]{2,1,0:T(8,128)(2,1)} copy(bf16[1,512,1280]{2,1,0:T(8,128)(2,1)S(1)} %bitcast.9) | data formatting | bytes 2621440
  69.3 0.0 copy-start.3
  69.3 1.1 %copy.17 = bf16[1,512,1280]{2,1,0:T(8,128)(2,1)} copy(bf16[1,512,1280]{2,1,0:T(8,128)(2,1)S(1)} %bitcast.8) | data formatting | bytes 2621440
  70.4 0.6 copy.18
  71.0 0.3 copy-done.3
  71.2 0.0 copy-start.2
  71.2 1.2 %copy.19 = bf16[1,1280,640]{2,1,0:T(8,128)(2,1)} copy(bf16[1,1280,640]{2,1,0:T(8,128)(2,1)S(1)} %bitcast.15) | data formatting | bytes 3276800
  72.4 0.9 %copy-done.2 = bf16[640,1280]{1,0:T(8,128)(2,1)S(1)} copy-done((bf16[640,1280]{1,0:T(8,128)(2,1)S(1)}, bf16[640,1280]{1,0:T(8,128)(2,1)}, u32[]{:S(2)}) %copy-start.2) | copy-done | bytes 1638424
  73.2 1.2 %copy.20 = bf16[1,640,1280]{2,1,0:T(8,128)(2,1)} copy(bf16[1,640,1280]{2,1,0:T(8,128)(2,1)S(1)} %bitcast.14) | data formatting | bytes 3276800
Async XLA Ops:
  1.8 1.3 %copy-start = (bf16[1,512,1280]{2,1,0:T(8,128)(2,1)S(1)}, bf16[1,512,1280]{2,1,0:T(8,128)(2,1)}, u32[]{:S(2)}) copy-start(bf16[1,512,1280]{2,1,0:T(8,128)(2,1)} %param.5) | copy-start | bytes 3932164
  3.1 1.3 %copy-start.1 = (bf16[1,512,1280]{2,1,0:T(8,128)(2,1)S(1)}, bf16[1,512,1280]{2,1,0:T(8,128)(2,1)}, u32[]{:S(2)}) copy-start(bf16[1,512,1280]{2,1,0:T(8,128)(2,1)} %param.9) | copy-start | bytes 3932164
  69.3 1.9 %copy-start.3 = (bf16[1280,640]{1,0:T(8,128)(2,1)S(1)}, bf16[1280,640]{1,0:T(8,128)(2,1)}, u32[]{:S(2)}) copy-start(bf16[1280,640]{1,0:T(8,128)(2,1)} %get-tuple-element.13) | copy-start | bytes 4915204
  71.2 2.0 %copy-start.2 = (bf16[640,1280]{1,0:T(8,128)(2,1)S(1)}, bf16[640,1280]{1,0:T(8,128)(2,1)}, u32[]{:S(2)}) copy-start(bf16[640,1280]{1,0:T(8,128)(2,1)} %get-tuple-element.14) | copy-start | bytes 4915204

commit v2 on v0

v2 whole, which is shorter than its diff:
```python
import math

import jax
import jax.numpy as jnp
from jax import lax
from jax.experimental import pallas as pl
from jax.experimental.pallas import tpu as pltpu
from jax.sharding import PartitionSpec as P

F32 = jnp.float32
BF16 = jnp.bfloat16
MESH = pl.DeviceIdType.MESH
SEQ = 8
YS = 4
XS = 4
ZS = 8
D = 1280
H = 640
T = 512
S = 64
VMEM = 52 * 1024 * 1024


def nn(a, b):
    return lax.dot_general(a, b, (((1,), (0,)), ((), ())), preferred_element_type=F32)


def nt(a, b):
    return lax.dot_general(a, b, (((1,), (1,)), ((), ())), preferred_element_type=F32)


def split(a):
    high = a.astype(BF16)
    return high, (a - high.astype(F32)).astype(BF16)


def block(a, g):
    rows = a[8 * g : 8 * g + 8]
    return jnp.concatenate([rows[:, :H], rows[:, H:]], axis=0)


def store_blocks(ref, a):
    for g in range(SEQ):
        ref[g % 2, g // 2] = block(a, g).astype(ref.dtype)


def load_blocks(ref):
    parts = [ref[g % 2, g // 2].astype(F32) for g in range(SEQ)]
    lo = jnp.concatenate([p[:8, :H] for p in parts], axis=0)
    hi = jnp.concatenate([p[8:, :H] for p in parts], axis=0)
    return jnp.concatenate([lo, hi], axis=1).astype(BF16)


def pair_rows(top, low):
    square = jnp.concatenate(
        [jnp.broadcast_to(top, (S, 128)), jnp.broadcast_to(low, (S, 128))], axis=0
    )
    return square.T[:8]


def columns(rows):
    return jnp.concatenate([rows] * 16, axis=0).T


def left(a, b):
    lane = lax.broadcasted_iota(jnp.int32, a.shape, 1)
    return jnp.where(lane < S, a, pltpu.roll(b, S, 1))


def merge(stats):
    lane = lax.broadcasted_iota(jnp.int32, (8, 128), 1)
    top = stats[0]
    for s in stats[1:]:
        top = jnp.maximum(top, s)
    total = jnp.zeros((8, 128), F32)
    weights = []
    for s in stats:
        w = jnp.exp(jnp.where(lane < S, s - top, 0.0))
        weights.append(w)
        total = total + pltpu.roll(s, S, 1) * w
    return jnp.where(lane < S, top, 0.0), total, weights


def kernel(
    tokens_hbm, router_hbm, w_in_hbm, w_out_hbm, grad_hbm,
    mixed_v, d_tok_v, d_rout_v, d_w_in_v, d_w_out_v,
    tok, rout, w_in, w_out, grad,
    rc0, rc1, rc2, rc3, rm0, rm1, rm2, rm3, ry0, ry1, ry2, ry3, rr0, rr1, rr2, rr3,
    es0, es1, es2, es3, er0, er1, er2, er3, ag0, ag1, ag2, ag3,
    st_send, st_mid, st_core, st_recv, weight,
    tc_send, tc_mid, tc_sum, ty_send, ty_recv, ty_sum, tz_send, tz_recv,
    in_sem, send_sem, recv_sem,
):
    rc, rm, ry, rr = (rc0, rc1, rc2, rc3), (rm0, rm1, rm2, rm3), (ry0, ry1, ry2, ry3), (rr0, rr1, rr2, rr3)
    es, er, ag = (es0, es1, es2, es3), (er0, er1, er2, er3), (ag0, ag1, ag2, ag3)
    me_s = lax.axis_index("seq")
    me_n = lax.axis_index("exp")
    y = me_s // 2
    core = lax.rem(me_s, 2)
    z = me_n // XS
    x = lax.rem(me_n, XS)
    twin = me_s + 1 - 2 * core
    partner = lax.rem(me_s - z + SEQ, SEQ)
    own = lax.rem(core + z, 2)
    away = 1 - own
    mine = partner // 2

    loads = [
        pltpu.make_async_copy(src, dst, in_sem.at[i])
        for i, (src, dst) in enumerate(
            ((router_hbm, rout), (tokens_hbm, tok), (grad_hbm, grad), (w_in_hbm, w_in), (w_out_hbm, w_out))
        )
    ]
    loads[0].start()
    loads[1].start()

    barrier = pltpu.get_barrier_semaphore()

    def greet(s, n):
        pl.semaphore_signal(barrier, inc=1, device_id=(s, n), device_id_type=MESH)

    def ex_peer(k):
        return XS * partner + k

    for k in range(XS):

        @pl.when(ex_peer(k) != me_n)
        def _():
            greet(me_s, ex_peer(k))

    def greet_z(k, carry):
        greet(me_s, XS * lax.rem(z + k, ZS) + x)
        return carry

    def yx_peer(k):
        return 2 * lax.rem(y + k // XS, YS) + core, XS * z + lax.rem(x + lax.rem(k, XS), XS)

    def greet_yx(k, carry):
        greet(*yx_peer(k))
        return carry

    lax.fori_loop(1, ZS, greet_z, 0)
    lax.fori_loop(1, YS * XS, greet_yx, 0)
    greet(twin, me_n)

    def send(src, dst, sem, s, n):
        pltpu.make_async_remote_copy(
            src_ref=src, dst_ref=dst, send_sem=send_sem.at[sem], recv_sem=recv_sem.at[sem],
            device_id=(s, n), device_id_type=MESH,
        ).start()

    def all_of(ref, sem):
        pltpu.make_async_copy(ref, ref, sem).wait()

    def arrived(ref, sem):
        all_of(ref, recv_sem.at[sem])

    def over_y(make):
        def step(k, carry):
            make(2 * lax.rem(y + k, YS) + core)
            return carry

        lax.fori_loop(1, YS, step, 0)

    def rs_core(i):
        send(rc[i].at[away], rm[i], 5 * i, twin, me_n)

    def rs_y_send(i):
        rr[i][y] = ry[i][mine]
        over_y(
            lambda s: send(
                ry[i].at[lax.rem(s - z + SEQ, SEQ) // 2], rr[i].at[y], 5 * i + 1, s, me_n
            )
        )

    def rs_y(i):
        arrived(rm[i], 5 * i)
        for k in range(YS):
            ry[i][k] = (rc[i][own, k].astype(F32) + rm[i][k].astype(F32)).astype(ry[i].dtype)
        rs_y_send(i)

    def rs_total(i):
        arrived(rr[i].at[pl.ds(0, YS - 1)], 5 * i + 1)
        total = rr[i][0].astype(F32)
        for k in range(1, YS):
            total = total + rr[i][k].astype(F32)
        return total

    def ex_start(i, total, extra=None):
        rows = [total[:8], total[8:]]
        if extra is not None:
            rows.append(extra)
        rows = jnp.concatenate(rows, axis=1)
        for k in range(XS):
            es[i][k] = rows[2 * k : 2 * k + 2]
        for k in range(XS):

            @pl.when(ex_peer(k) != me_n)
            def _():
                send(es[i].at[k], er[i].at[x], 5 * i + 2, me_s, ex_peer(k))

            @pl.when(ex_peer(k) == me_n)
            def _():
                er[i][x] = es[i][k]

    def ex_rows(i):
        @pl.when(partner != z)
        def _():
            arrived(er[i], 5 * i + 2)

        @pl.when(partner == z)
        def _():
            arrived(er[i].at[pl.ds(0, XS - 1)], 5 * i + 2)

        return jnp.concatenate([er[i][k] for k in range(XS)], axis=0)

    def ag_start(i, rows):
        piece = jnp.concatenate([rows[:, :H], rows[:, H:D]], axis=0)
        if rows.shape[1] > D:
            value = rows[:, D:]
            high, rest = split(value)
            middle, low = split(value - high.astype(F32))
            lane = lax.broadcasted_iota(jnp.int32, (8, 128), 1)
            value = jnp.where(
                lane == 0,
                high.astype(F32),
                jnp.where(lane == 1, middle.astype(F32), jnp.where(lane == 2, low.astype(F32), 0.0)),
            )
            piece = jnp.concatenate(
                [piece, jnp.concatenate([value, jnp.zeros((8, 128), F32)], axis=0)], axis=1
            )
        ag[i][own, mine] = piece.astype(BF16)
        over_y(lambda s: send(ag[i].at[own, mine], ag[i].at[own, mine], 5 * i + 3, s, me_n))

    def ag_core(i):
        arrived(ag[i].at[0, pl.ds(0, YS - 1)], 5 * i + 3)
        send(ag[i].at[own], ag[i].at[own], 5 * i + 4, twin, me_n)

    def ag_finish(i):
        arrived(ag[i].at[0], 5 * i + 4)
        return load_blocks(ag[i])

    loads[0].wait()
    loads[1].wait()
    for load in loads[2:]:
        load.start()
    router_t = rout[...]
    logits = nt(router_t, tok[...])
    own_top = jnp.max(logits, axis=1, keepdims=True)
    own_exp = jnp.exp(logits - own_top)
    st_send[...] = pair_rows(own_top, jnp.sum(own_exp, axis=1, keepdims=True))
    exp_high, exp_low = split(own_exp)
    store_blocks(rc[1], nn(exp_high, tok[...]) + nn(exp_low, tok[...]))

    @pl.when(partner != z)
    def _():
        pl.semaphore_wait(barrier, 1 + YS * XS - 1 + ZS - 1 + XS)

    @pl.when(partner == z)
    def _():
        pl.semaphore_wait(barrier, 1 + YS * XS - 1 + ZS - 1 + XS - 1)

    rs_core(1)
    send(st_send, st_mid, 20, twin, me_n)
    row_exp = jnp.exp(logits - jnp.max(logits, axis=0, keepdims=True))
    combine = row_exp / jnp.sum(row_exp, axis=0, keepdims=True)
    loads[2].wait()
    store_blocks(rc[0], nn(combine.astype(BF16), grad[...]))
    rs_core(0)

    arrived(st_mid, 20)
    top, total, (w_own, w_mid) = merge([st_send[...], st_mid[...]])
    st_core[...] = left(top, total)
    weight[...] = columns(left(w_own, w_mid))
    arrived(rm[1], 5)
    for k in range(YS):
        g = pl.multiple_of(8 * (own + 2 * k), 8)
        a = weight[pl.ds(g, 8)]
        b = weight[pl.ds(S + g, 8)]
        a = jnp.concatenate([jnp.concatenate([a] * 5, axis=1)] * 2, axis=0)
        b = jnp.concatenate([jnp.concatenate([b] * 5, axis=1)] * 2, axis=0)
        ry[1][k] = rc[1][own, k] * a + rm[1][k] * b
    st_recv[y] = st_core[...]
    over_y(lambda s: send(st_core, st_recv.at[y], 21, s, me_n))
    rs_y_send(1)
    rs_y(0)

    arrived(st_recv.at[pl.ds(0, YS - 1)], 21)
    stats = [st_recv[k] for k in range(YS)]
    top, total, ws = merge(stats)
    w = [v / total for v in ws]
    weight[...] = columns(left(w[0], w[1]))
    g = pl.multiple_of(8 * partner, 8)
    w0, w1 = weight[pl.ds(g, 8)], weight[pl.ds(S + g, 8)]
    weight[...] = columns(left(w[2], w[3]))
    w2, w3 = weight[pl.ds(g, 8)], weight[pl.ds(S + g, 8)]
    arrived(rr[1].at[pl.ds(0, YS - 1)], 6)
    total_in = jnp.zeros((16, H), F32)
    for k, v in enumerate((w0, w1, w2, w3)):
        total_in = total_in + rr[1][k] * jnp.concatenate([jnp.concatenate([v] * 5, axis=1)] * 2, axis=0)
    ex_start(1, total_in)
    ex_start(0, rs_total(0))
    scale = columns(left(jnp.exp(st_send[...] - top) / total, total))[:S, :1]
    dispatch = own_exp * scale

    rows_1 = ex_rows(1)
    ag_start(1, rows_1)
    ag_start(0, ex_rows(0))
    ag_core(1)
    ag_core(0)

    loads[3].wait()
    rows = ag_finish(1)
    hidden = nn(rows, w_in[...])
    cdf = 0.5 * (1.0 + lax.erf(hidden * (1.0 / math.sqrt(2.0))))
    act = hidden * cdf
    loads[4].wait()
    store_blocks(rc[3], nn(act.astype(BF16), w_out[...]))
    rs_core(3)
    pdf = jnp.exp(-0.5 * hidden * hidden) * (1.0 / math.sqrt(2.0 * math.pi))
    slope = cdf + hidden * pdf
    d_rows = ag_finish(0)
    d_hidden_b = (nt(d_rows, w_out[...]) * slope).astype(BF16)
    store_blocks(rc[2], nt(d_hidden_b, w_in[...]))
    rs_core(2)

    rs_y(3)
    rs_y(2)
    act_t = act.T.astype(BF16)
    for k in range(5):
        part = slice(128 * k, 128 * k + 128)
        d_w_out_v[part] = nn(act_t[part], d_rows).astype(BF16)
    ex_start(3, rs_total(3))
    total = rs_total(2).astype(BF16).astype(F32)
    column = jnp.sum(total[:8] * rows_1[:, :H] + total[8:] * rows_1[:, H:], axis=1, keepdims=True)
    ex_start(2, total, jnp.broadcast_to(column, (8, 128)))
    rows_t = rows.astype(F32).T.astype(BF16)
    for k in range(10):
        part = slice(128 * k, 128 * k + 128)
        d_w_in_v[part] = nn(rows_t[part], d_hidden_b).astype(BF16)
    ag_start(3, ex_rows(3))
    ag_start(2, ex_rows(2))
    ag_core(3)
    ag_core(2)

    slots_out = ag_finish(3)
    d_combine = nt(slots_out, grad[...])
    d_logit_c = combine * (d_combine - jnp.sum(combine * d_combine, axis=0, keepdims=True))
    d_slots = ag_finish(2)
    column = jnp.concatenate(
        [ag[2][g % 2, g // 2, :8, H:].astype(F32) for g in range(SEQ)], axis=0
    )
    column = jnp.sum(column, axis=1, keepdims=True)
    d_dispatch = nt(d_slots, tok[...])
    d_logit = d_logit_c + dispatch * (d_dispatch - column)

    d_router_t = nn(d_logit.astype(BF16), tok[...])
    pair = jnp.concatenate([d_router_t, pltpu.roll(d_router_t, D - 80, 1)], axis=0).T
    for k in range(SEQ):
        tc_send[k % 2, k // 2] = pair[160 * k : 160 * k + 80]
    send(tc_send.at[1 - core], tc_mid, 22, twin, me_n)
    combine_t = combine.T.astype(BF16)
    for k in range(4):
        part = slice(128 * k, 128 * k + 128)
        mixed_v[part] = nn(combine_t[part], slots_out).astype(BF16)
    arrived(tc_mid, 22)
    for k in range(YS):
        tc_sum[k] = tc_send[core, k] + tc_mid[k]
    for k in range(YS):
        for j in range(XS):
            for i in range(4):
                ty_send[k, j, 5 * i : 5 * i + 5] = tc_sum[k, 20 * i + 5 * j : 20 * i + 5 * j + 5]
    ty_recv[XS * y + x] = ty_send[y, x]

    def send_yx(k, carry):
        s, n = yx_peer(k)
        send(ty_send.at[s // 2, lax.rem(n, XS)], ty_recv.at[XS * y + x], 23, s, n)
        return carry

    lax.fori_loop(1, YS * XS, send_yx, 0)
    weights = jnp.concatenate([dispatch, d_logit], axis=0).T.astype(BF16)
    values = jnp.concatenate([d_slots, router_t], axis=0)
    for k in range(4):
        part = slice(128 * k, 128 * k + 128)
        d_tok_v[part] = nn(weights[part], values).astype(BF16)
    arrived(ty_recv.at[pl.ds(0, YS * XS - 1)], 23)
    total = ty_recv[0]
    for k in range(1, YS * XS):
        total = total + ty_recv[k]
    ty_sum[...] = total
    for k in range(4):
        tz_send[k] = ty_sum[5 * k : 5 * k + 8]
    tz_recv[z] = tz_send[lax.rem(z, 4)]

    def send_z(k, carry):
        to = lax.rem(z + k, ZS)
        send(tz_send.at[lax.rem(to, 4)], tz_recv.at[z], 24, me_s, XS * to + x)
        return carry

    lax.fori_loop(1, ZS, send_z, 0)
    arrived(tz_recv.at[pl.ds(0, ZS - 1)], 24)
    total = tz_recv[0]
    for k in range(1, ZS):
        total = total + tz_recv[k]
    total = jnp.where(z >= 4, pltpu.roll(total, S, 1), total)
    d_rout_v[...] = total[:5, :S]

    for i in range(4):
        all_of(rm[i], send_sem.at[5 * i])
        all_of(rr[i].at[pl.ds(0, YS - 1)], send_sem.at[5 * i + 1])

        @pl.when(partner != z)
        def _():
            all_of(er[i], send_sem.at[5 * i + 2])

        @pl.when(partner == z)
        def _():
            all_of(er[i].at[pl.ds(0, XS - 1)], send_sem.at[5 * i + 2])

        all_of(ag[i].at[0, pl.ds(0, YS - 1)], send_sem.at[5 * i + 3])
        all_of(ag[i].at[0], send_sem.at[5 * i + 4])
    all_of(st_mid, send_sem.at[20])
    all_of(st_recv.at[pl.ds(0, YS - 1)], send_sem.at[21])
    all_of(tc_mid, send_sem.at[22])
    all_of(ty_recv.at[pl.ds(0, YS * XS - 1)], send_sem.at[23])
    all_of(tz_recv.at[pl.ds(0, ZS - 1)], send_sem.at[24])


def store(a0, a1, a2, a3, a4, b0, b1, b2, b3, b4, sem):
    copies = [
        pltpu.make_async_copy(a, b, sem.at[i])
        for i, (a, b) in enumerate(((a0, b0), (a1, b1), (a2, b2), (a3, b3), (a4, b4)))
    ]
    for copy in copies:
        copy.start()
    for copy in copies:
        copy.wait()


def shards(tokens, router, w_in, w_out, grad_out):
    any_space = pl.BlockSpec(memory_space=pl.ANY)
    dma = pltpu.SemaphoreType.DMA
    vmem = pltpu.VMEM
    kinds = (BF16, F32, BF16, BF16)
    wide = (0, 0, 128, 0)
    results = pl.pallas_call(
        kernel,
        out_shape=(
            vmem((T, D), BF16),
            vmem((T, D), BF16),
            vmem((5, S), F32),
            vmem((D, H), BF16),
            vmem((H, D), BF16),
        ),
        in_specs=[any_space] * 5,
        out_specs=[pl.BlockSpec(memory_space=vmem)] * 5,
        scratch_shapes=[
            vmem((T, D), BF16),
            vmem((S, D), BF16),
            vmem((D, H), BF16),
            vmem((H, D), BF16),
            vmem((T, D), BF16),
            *[vmem((2, 4, 16, H), k) for k in kinds],
            *[vmem((4, 16, H), k) for k in kinds],
            *[vmem((4, 16, H), k) for k in kinds],
            *[vmem((4, 16, H), k) for k in kinds],
            *[vmem((XS, 2, D + w), F32) for w in wide],
            *[vmem((XS, 2, D + w), F32) for w in wide],
            *[vmem((2, 4, 16, H + w), BF16) for w in wide],
            vmem((8, 128), F32),
            vmem((8, 128), F32),
            vmem((8, 128), F32),
            vmem((YS, 8, 128), F32),
            vmem((128, 128), F32),
            vmem((2, YS, 80, 128), F32),
            vmem((YS, 80, 128), F32),
            vmem((YS, 80, 128), F32),
            vmem((YS, XS, 24, 128), F32),
            vmem((YS * XS, 24, 128), F32),
            vmem((24, 128), F32),
            vmem((4, 8, 128), F32),
            vmem((ZS, 8, 128), F32),
            dma((5,)), dma((25,)), dma((25,)),
        ],
        compiler_params=pltpu.CompilerParams(
            collective_id=0, has_side_effects=True, vmem_limit_bytes=VMEM
        ),
    )(tokens[0], router.T, w_in[0], w_out[0], grad_out[0])
    mixed, d_tokens, d_router, d_w_in, d_w_out = pl.pallas_call(
        store,
        out_shape=tuple(jax.ShapeDtypeStruct(r.shape, r.dtype) for r in results),
        in_specs=[pl.BlockSpec(memory_space=vmem)] * 5,
        out_specs=[any_space] * 5,
        scratch_shapes=[dma((5,))],
        compiler_params=pltpu.CompilerParams(vmem_limit_bytes=4 * 1024 * 1024),
    )(*results)
    return mixed[None], d_tokens[None], d_router, d_w_in[None], d_w_out[None]


def solution(mesh):
    in_specs = (
        P("exp", "seq", None),
        P(),
        P("exp", None, "seq"),
        P("exp", "seq", None),
        P("exp", "seq", None),
    )
    out_specs = (
        P("exp", "seq", None),
        P("exp", "seq", None),
        P(("seq", "exp"), None),
        P("exp", None, "seq"),
        P("exp", "seq", None),
    )
    return jax.shard_map(shards, mesh=mesh, in_specs=in_specs, out_specs=out_specs, check_vma=False)
```

time: 488 us -> 60.2 us (0.12)
  waiting for transfers between devices: 317 us -> 0 us
  blocking collectives: 72.6 us -> 0 us
  Pallas kernels: 0 us -> 58.8 us
  starting transfers between devices: 30.7 us -> 0 us
  matrix products: 30.5 us -> 0 us
  local copies, waits for them, and re-layouts: 17.4 us -> 0 us
  between operations: 14.2 us -> 0.64 us
    unnamed x3 -> x0, waiting for transfers between devices: 234 us -> none
    psum x1 -> x0, waiting for transfers between devices: 61.8 us -> none  [from_experts(): summed = lax.psum(partial_value.astype(jnp.bfloat16), 'seq')]
    pallas_call x0 -> x2, Pallas kernels: none -> 58.8 us  [the longest x1 56.2 us: shards(): pl.pallas_call(kernel, out_shape=(vmem((T, D), BF16), vmem((T, D), BF16),...]
    psum x3 -> x0, blocking collectives: 57.6 us -> none  [the longest x1 27.4 us: to_experts(): summed = lax.psum(partial_value, 'seq').astype(jnp.bfloat16)]
    all_to_all x4 -> x0, starting transfers between devices: 30.6 us -> none  [the longest x2 15.9 us: to_experts(): lax.all_to_all(summed, 'exp', split_axis=1, concat_axis=0, tiled=True)]
    dot_general x15 -> x0, matrix products: 30.5 us -> none  [the longest x1 3.52 us: shards(): lax.dot_general(d_logit_b, router, (((0,), (1,)), ((), ())), preferred_el...]
    all_to_all x4 -> x0, waiting for transfers between devices: 21.4 us -> none  [the longest x2 11.2 us: to_experts(): lax.all_to_all(summed, 'exp', split_axis=1, concat_axis=0, tiled=True)]
    pmax x1 -> x0, blocking collectives: 15 us -> none  [shards(): col_top = lax.pmax(jnp.max(logits, axis=1), 'seq')]
  transfers between devices with their start and end apart: 6 -> 0, of which waited for: 6 -> 0; matrix products, arithmetic and copies ran while one was open for 5% -> 0% of each run, Pallas kernels for 0% -> 0%
where the time goes in v2:
time: 60.2 us; the launch traced here: 59.4 us
  Pallas kernels  58.8 us (98%)
  between operations  0.64 us (1%)
    pallas_call x1, Pallas kernels, shards(): pl.pallas_call(kernel, out_shape=(vmem((T, D), BF16), vmem((T, D), BF16),...  56.2 us
    pallas_call x1, Pallas kernels, shards(): pl.pallas_call(store, out_shape=tuple((jax.ShapeDtypeStruct(r.shape, r.dt...  2.62 us

profile of v2, /device:TPU:1, one launch (start us, length us, event | category | flops | bytes accessed | tf_op | source)
XLA Modules:
  0.0 59.4 jit_solution(9795793687768493958)
XLA Ops:
  0.6 56.2 %shard_map.92 = (bf16[512,1280]{1,0:T(8,128)(2,1)S(1)}, bf16[512,1280]{1,0:T(8,128)(2,1)S(1)}, f32[5,64]{1,0:T(8,128)S(1)}, bf16[1280,640]{1,0:T(8,128)(2,1)S(1)}, bf16[640,1280]{1,0:T(8,128)(2,1)S(1)}) custom-call(bf16[512,1280]{1,0:T(8,128)(2,1)} %bitcast.11, bf16[64,1280]{1,0:T(8,128)(2,1)} %bitcast.13, bf16[1280,640]{1,0:T(8,128)(2,1)} %bitcast.9, ...), custom_call_target="tpu_custom_call" | custom-call | tf_op jit(solution)/shard_map/pallas_call | solution.py:446
  56.8 2.6 %shard_map.93 = (bf16[512,1280]{1,0:T(8,128)(2,1)}, bf16[512,1280]{1,0:T(8,128)(2,1)}, f32[5,64]{1,0:T(8,128)}, bf16[1280,640]{1,0:T(8,128)(2,1)}, bf16[640,1280]{1,0:T(8,128)(2,1)}) custom-call(bf16[512,1280]{1,0:T(8,128)(2,1)S(1)} %get-tuple-element.15.a0, bf16[512,1280]{1,0:T(8,128)(2,1)S(1)} %get-tuple-element.16.a1, f32[5,64]{1,0:T(8,128)S(1)} %get-tuple-element.17.a2, ...), custom_call_target="tpu_custom_call" | custom-call | tf_op jit(solution)/shard_map/pallas_call | solution.py:489

commit v3 on v2

--- a/solution.py
+++ b/solution.py
@@ -14,6 +14,8 @@
 YS = 4
 XS = 4
 ZS = 8
+DIRECT = (0, 2)
+NEAR = (1, 2, ZS - 2, ZS - 1)
 D = 1280
 H = 640
 T = 512
@@ -34,6 +36,16 @@
     return high, (a - high.astype(F32)).astype(BF16)
 
 
+def thirds(column):
+    value = jnp.broadcast_to(column, (8, 128))
+    high, rest = split(value)
+    middle, low = split(value - high.astype(F32))
+    lane = lax.broadcasted_iota(jnp.int32, (8, 128), 1)
+    value = jnp.where(lane == 2, low.astype(F32), 0.0)
+    value = jnp.where(lane == 1, middle.astype(F32), value)
+    return jnp.where(lane == 0, high.astype(F32), value)
+
+
 def block(a, g):
     rows = a[8 * g : 8 * g + 8]
     return jnp.concatenate([rows[:, :H], rows[:, H:]], axis=0)
@@ -45,7 +57,7 @@
 
 
 def load_blocks(ref):
-    parts = [ref[g % 2, g // 2].astype(F32) for g in range(SEQ)]
+    parts = [ref[4 * (g % 2) + g // 2].astype(F32) for g in range(SEQ)]
     lo = jnp.concatenate([p[:8, :H] for p in parts], axis=0)
     hi = jnp.concatenate([p[8:, :H] for p in parts], axis=0)
     return jnp.concatenate([lo, hi], axis=1).astype(BF16)
@@ -88,8 +100,8 @@
     rc0, rc1, rc2, rc3, rm0, rm1, rm2, rm3, ry0, ry1, ry2, ry3, rr0, rr1, rr2, rr3,
     es0, es1, es2, es3, er0, er1, er2, er3, ag0, ag1, ag2, ag3,
     st_send, st_mid, st_core, st_recv, weight,
-    tc_send, tc_mid, tc_sum, ty_send, ty_recv, ty_sum, tz_send, tz_recv,
-    in_sem, send_sem, recv_sem,
+    tc_send, tc_mid, tc_sum, ty_send, ty_recv, tz_send, tz_recv,
+    in_sem, send_sem, recv_sem, hello,
 ):
     rc, rm, ry, rr = (rc0, rc1, rc2, rc3), (rm0, rm1, rm2, rm3), (ry0, ry1, ry2, ry3), (rr0, rr1, rr2, rr3)
     es, er, ag = (es0, es1, es2, es3), (er0, er1, er2, er3), (ag0, ag1, ag2, ag3)
@@ -108,11 +120,18 @@
     loads = [
         pltpu.make_async_copy(src, dst, in_sem.at[i])
         for i, (src, dst) in enumerate(
-            ((router_hbm, rout), (tokens_hbm, tok), (grad_hbm, grad), (w_in_hbm, w_in), (w_out_hbm, w_out))
+            ((router_hbm, rout), (grad_hbm, grad), (w_in_hbm, w_in), (w_out_hbm, w_out))
         )
     ]
+    pieces = [
+        pltpu.make_async_copy(
+            tokens_hbm.at[pl.ds(128 * k, 128)], tok.at[pl.ds(128 * k, 128)], in_sem.at[4 + k]
+        )
+        for k in range(4)
+    ]
     loads[0].start()
-    loads[1].start()
+    for piece in pieces:
+        piece.start()
 
     barrier = pltpu.get_barrier_semaphore()
 
@@ -122,26 +141,22 @@
     def ex_peer(k):
         return XS * partner + k
 
-    for k in range(XS):
-
-        @pl.when(ex_peer(k) != me_n)
-        def _():
-            greet(me_s, ex_peer(k))
-
-    def greet_z(k, carry):
-        greet(me_s, XS * lax.rem(z + k, ZS) + x)
-        return carry
-
     def yx_peer(k):
         return 2 * lax.rem(y + k // XS, YS) + core, XS * z + lax.rem(x + lax.rem(k, XS), XS)
 
-    def greet_yx(k, carry):
-        greet(*yx_peer(k))
-        return carry
-
-    lax.fori_loop(1, ZS, greet_z, 0)
-    lax.fori_loop(1, YS * XS, greet_yx, 0)
+    along_x = [XS * z + lax.rem(x + k, XS) for k in range(1, XS)]
+    along_z = [XS * lax.rem(z + k, ZS) + x for k in NEAR]
+    for k in range(1, YS):
+        greet(2 * lax.rem(y + k, YS) + core, me_n)
+    for n in along_x + along_z:
+        greet(me_s, n)
     greet(twin, me_n)
+
+    def pass_on(sem, devices):
+        for n in devices:
+            pl.semaphore_signal(
+                hello.at[sem], inc=1, device_id=(me_s, n), device_id_type=MESH
+            )
 
     def send(src, dst, sem, s, n):
         pltpu.make_async_remote_copy(
@@ -192,7 +207,7 @@
             rows.append(extra)
         rows = jnp.concatenate(rows, axis=1)
         for k in range(XS):
-            es[i][k] = rows[2 * k : 2 * k + 2]
+            es[i][k] = rows[2 * k : 2 * k + 2].astype(es[i].dtype)
         for k in range(XS):
 
             @pl.when(ex_peer(k) != me_n)
@@ -212,37 +227,40 @@
         def _():
             arrived(er[i].at[pl.ds(0, XS - 1)], 5 * i + 2)
 
-        return jnp.concatenate([er[i][k] for k in range(XS)], axis=0)
+        return jnp.concatenate([er[i][k].astype(F32) for k in range(XS)], axis=0)
 
     def ag_start(i, rows):
         piece = jnp.concatenate([rows[:, :H], rows[:, H:D]], axis=0)
         if rows.shape[1] > D:
-            value = rows[:, D:]
-            high, rest = split(value)
-            middle, low = split(value - high.astype(F32))
-            lane = lax.broadcasted_iota(jnp.int32, (8, 128), 1)
-            value = jnp.where(
-                lane == 0,
-                high.astype(F32),
-                jnp.where(lane == 1, middle.astype(F32), jnp.where(lane == 2, low.astype(F32), 0.0)),
-            )
-            piece = jnp.concatenate(
-                [piece, jnp.concatenate([value, jnp.zeros((8, 128), F32)], axis=0)], axis=1
-            )
-        ag[i][own, mine] = piece.astype(BF16)
-        over_y(lambda s: send(ag[i].at[own, mine], ag[i].at[own, mine], 5 * i + 3, s, me_n))
+            extra = jnp.concatenate([rows[:, D:], jnp.zeros((8, 128), F32)], axis=0)
+            piece = jnp.concatenate([piece, extra], axis=1)
+        ag[i][4 * own + mine] = piece.astype(BF16)
+        if i in DIRECT:
+            for k in range(1, SEQ):
+                send(
+                    ag[i].at[4 * own + mine], ag[i].at[4 * own + mine], 5 * i + 3, lax.rem(me_s + k, SEQ), me_n
+                )
+        else:
+            over_y(lambda s: send(ag[i].at[4 * own + mine], ag[i].at[4 * own + mine], 5 * i + 3, s, me_n))
 
     def ag_core(i):
-        arrived(ag[i].at[0, pl.ds(0, YS - 1)], 5 * i + 3)
-        send(ag[i].at[own], ag[i].at[own], 5 * i + 4, twin, me_n)
+        if i in DIRECT:
+            return
+        arrived(ag[i].at[pl.ds(0, YS - 1)], 5 * i + 3)
+        half = ag[i].at[pl.ds(pl.multiple_of(4 * own, 4), 4)]
+        send(half, half, 5 * i + 4, twin, me_n)
 
     def ag_finish(i):
-        arrived(ag[i].at[0], 5 * i + 4)
+        if i in DIRECT:
+            arrived(ag[i].at[pl.ds(0, SEQ - 1)], 5 * i + 3)
+        else:
+            arrived(ag[i].at[pl.ds(0, YS)], 5 * i + 4)
         return load_blocks(ag[i])
 
     loads[0].wait()
-    loads[1].wait()
-    for load in loads[2:]:
+    for piece in pieces:
+        piece.wait()
+    for load in loads[1:]:
         load.start()
     router_t = rout[...]
     logits = nt(router_t, tok[...])
@@ -252,19 +270,13 @@
     exp_high, exp_low = split(own_exp)
     store_blocks(rc[1], nn(exp_high, tok[...]) + nn(exp_low, tok[...]))
 
-    @pl.when(partner != z)
-    def _():
-        pl.semaphore_wait(barrier, 1 + YS * XS - 1 + ZS - 1 + XS)
-
-    @pl.when(partner == z)
-    def _():
-        pl.semaphore_wait(barrier, 1 + YS * XS - 1 + ZS - 1 + XS - 1)
-
+    pl.semaphore_wait(barrier, 1 + YS - 1 + XS - 1 + len(NEAR))
     rs_core(1)
     send(st_send, st_mid, 20, twin, me_n)
+    pass_on(0, along_x + along_z)
     row_exp = jnp.exp(logits - jnp.max(logits, axis=0, keepdims=True))
     combine = row_exp / jnp.sum(row_exp, axis=0, keepdims=True)
-    loads[2].wait()
+    loads[1].wait()
     store_blocks(rc[0], nn(combine.astype(BF16), grad[...]))
     rs_core(0)
 
@@ -284,6 +296,8 @@
     over_y(lambda s: send(st_core, st_recv.at[y], 21, s, me_n))
     rs_y_send(1)
     rs_y(0)
+    pl.semaphore_wait(hello.at[0], XS - 1 + len(NEAR))
+    pass_on(1, along_z)
 
     arrived(st_recv.at[pl.ds(0, YS - 1)], 21)
     stats = [st_recv[k] for k in range(YS)]
@@ -298,6 +312,7 @@
     total_in = jnp.zeros((16, H), F32)
     for k, v in enumerate((w0, w1, w2, w3)):
         total_in = total_in + rr[1][k] * jnp.concatenate([jnp.concatenate([v] * 5, axis=1)] * 2, axis=0)
+    pl.semaphore_wait(hello.at[1], len(NEAR))
     ex_start(1, total_in)
     ex_start(0, rs_total(0))
     scale = columns(left(jnp.exp(st_send[...] - top) / total, total))[:S, :1]
@@ -309,12 +324,12 @@
     ag_core(1)
     ag_core(0)
 
-    loads[3].wait()
+    loads[2].wait()
     rows = ag_finish(1)
     hidden = nn(rows, w_in[...])
     cdf = 0.5 * (1.0 + lax.erf(hidden * (1.0 / math.sqrt(2.0))))
     act = hidden * cdf
-    loads[4].wait()
+    loads[3].wait()
     store_blocks(rc[3], nn(act.astype(BF16), w_out[...]))
     rs_core(3)
     pdf = jnp.exp(-0.5 * hidden * hidden) * (1.0 / math.sqrt(2.0 * math.pi))
@@ -333,7 +348,7 @@
     ex_start(3, rs_total(3))
     total = rs_total(2).astype(BF16).astype(F32)
     column = jnp.sum(total[:8] * rows_1[:, :H] + total[8:] * rows_1[:, H:], axis=1, keepdims=True)
-    ex_start(2, total, jnp.broadcast_to(column, (8, 128)))
+    ex_start(2, total, thirds(column))
     rows_t = rows.astype(F32).T.astype(BF16)
     for k in range(10):
         part = slice(128 * k, 128 * k + 128)
@@ -348,7 +363,7 @@
     d_logit_c = combine * (d_combine - jnp.sum(combine * d_combine, axis=0, keepdims=True))
     d_slots = ag_finish(2)
     column = jnp.concatenate(
-        [ag[2][g % 2, g // 2, :8, H:].astype(F32) for g in range(SEQ)], axis=0
+        [ag[2][4 * (g % 2) + g // 2, :8, H:].astype(F32) for g in range(SEQ)], axis=0
     )
     column = jnp.sum(column, axis=1, keepdims=True)
     d_dispatch = nt(d_slots, tok[...])
@@ -368,8 +383,8 @@
         tc_sum[k] = tc_send[core, k] + tc_mid[k]
     for k in range(YS):
         for j in range(XS):
-            for i in range(4):
-                ty_send[k, j, 5 * i : 5 * i + 5] = tc_sum[k, 20 * i + 5 * j : 20 * i + 5 * j + 5]
+            for i in range(5):
+                ty_send[k, j, i] = tc_sum[k, pl.ds(5 * j + i, 4, stride=20), :]
     ty_recv[XS * y + x] = ty_send[y, x]
 
     def send_yx(k, carry):
@@ -387,14 +402,18 @@
     total = ty_recv[0]
     for k in range(1, YS * XS):
         total = total + ty_recv[k]
-    ty_sum[...] = total
-    for k in range(4):
-        tz_send[k] = ty_sum[5 * k : 5 * k + 8]
-    tz_recv[z] = tz_send[lax.rem(z, 4)]
+    tz_send[...] = jnp.zeros((ZS, 4, 128), F32)
+    for k in range(3):
+        first = total[2 * k]
+        second = total[2 * k + 1] if k < 2 else jnp.zeros((4, 128), F32)
+        for half, packed in enumerate((left(first, second), left(pltpu.roll(first, S, 1), pltpu.roll(second, S, 1)))):
+            for i in range(4):
+                tz_send[4 * half + i, k : k + 1] = packed[i : i + 1]
+    tz_recv[z] = tz_send[z]
 
     def send_z(k, carry):
         to = lax.rem(z + k, ZS)
-        send(tz_send.at[lax.rem(to, 4)], tz_recv.at[z], 24, me_s, XS * to + x)
+        send(tz_send.at[to], tz_recv.at[z], 24, me_s, XS * to + x)
         return carry
 
     lax.fori_loop(1, ZS, send_z, 0)
@@ -402,8 +421,9 @@
     total = tz_recv[0]
     for k in range(1, ZS):
         total = total + tz_recv[k]
-    total = jnp.where(z >= 4, pltpu.roll(total, S, 1), total)
-    d_rout_v[...] = total[:5, :S]
+    other = pltpu.roll(total, S, 1)
+    for k in range(5):
+        d_rout_v[k : k + 1] = (other if k % 2 else total)[k // 2 : k // 2 + 1, :S]
 
     for i in range(4):
         all_of(rm[i], send_sem.at[5 * i])
@@ -417,8 +437,11 @@
         def _():
             all_of(er[i].at[pl.ds(0, XS - 1)], send_sem.at[5 * i + 2])
 
-        all_of(ag[i].at[0, pl.ds(0, YS - 1)], send_sem.at[5 * i + 3])
-        all_of(ag[i].at[0], send_sem.at[5 * i + 4])
+        if i in DIRECT:
+            all_of(ag[i].at[pl.ds(0, SEQ - 1)], send_sem.at[5 * i + 3])
+        else:
+            all_of(ag[i].at[pl.ds(0, YS - 1)], send_sem.at[5 * i + 3])
+            all_of(ag[i].at[pl.ds(0, YS)], send_sem.at[5 * i + 4])
     all_of(st_mid, send_sem.at[20])
     all_of(st_recv.at[pl.ds(0, YS - 1)], send_sem.at[21])
     all_of(tc_mid, send_sem.at[22])
@@ -464,9 +487,9 @@
             *[vmem((4, 16, H), k) for k in kinds],
             *[vmem((4, 16, H), k) for k in kinds],
             *[vmem((4, 16, H), k) for k in kinds],
-            *[vmem((XS, 2, D + w), F32) for w in wide],
-            *[vmem((XS, 2, D + w), F32) for w in wide],
-            *[vmem((2, 4, 16, H + w), BF16) for w in wide],
+            *[vmem((XS, 2, D + w), k) for w, k in zip(wide, kinds)],
+            *[vmem((XS, 2, D + w), k) for w, k in zip(wide, kinds)],
+            *[vmem((SEQ, 16, H + w), BF16) for w in wide],
             vmem((8, 128), F32),
             vmem((8, 128), F32),
             vmem((8, 128), F32),
@@ -475,12 +498,11 @@
             vmem((2, YS, 80, 128), F32),
             vmem((YS, 80, 128), F32),
             vmem((YS, 80, 128), F32),
-            vmem((YS, XS, 24, 128), F32),
-            vmem((YS * XS, 24, 128), F32),
-            vmem((24, 128), F32),
-            vmem((4, 8, 128), F32),
-            vmem((ZS, 8, 128), F32),
-            dma((5,)), dma((25,)), dma((25,)),
+            vmem((YS, XS, 5, 4, 128), F32),
+            vmem((YS * XS, 5, 4, 128), F32),
+            vmem((ZS, 4, 128), F32),
+            vmem((ZS, 4, 128), F32),
+            dma((8,)), dma((25,)), dma((25,)), pltpu.SemaphoreType.REGULAR((2,)),
         ],
         compiler_params=pltpu.CompilerParams(
             collective_id=0, has_side_effects=True, vmem_limit_bytes=VMEM

time: 60.2 us -> 59 us (0.980)
  Pallas kernels: 58.8 us -> 58.1 us
    pallas_call x1, Pallas kernels: 56.2 us -> 55.5 us  [shards(): pl.pallas_call(kernel, out_shape=(vmem((T, D), BF16), vmem((T, D), BF16),...]
where the time goes in v3:
time: 59 us; the launch traced here: 58.8 us
  Pallas kernels  58.1 us (98%)
  between operations  0.64 us (1%)
    pallas_call x1, Pallas kernels, shards(): pl.pallas_call(kernel, out_shape=(vmem((T, D), BF16), vmem((T, D), BF16),...  55.5 us
    pallas_call x1, Pallas kernels, shards(): pl.pallas_call(store, out_shape=tuple((jax.ShapeDtypeStruct(r.shape, r.dt...  2.62 us

profile of v3, /device:TPU:1, one launch (start us, length us, event | category | flops | bytes accessed | tf_op | source)
XLA Modules:
  0.0 58.8 jit_solution(5109338092239672198)
XLA Ops:
  0.6 55.5 %shard_map.92 = (bf16[512,1280]{1,0:T(8,128)(2,1)S(1)}, bf16[512,1280]{1,0:T(8,128)(2,1)S(1)}, f32[5,64]{1,0:T(8,128)S(1)}, bf16[1280,640]{1,0:T(8,128)(2,1)S(1)}, bf16[640,1280]{1,0:T(8,128)(2,1)S(1)}) custom-call(bf16[512,1280]{1,0:T(8,128)(2,1)} %bitcast.11, bf16[64,1280]{1,0:T(8,128)(2,1)} %bitcast.13, bf16[1280,640]{1,0:T(8,128)(2,1)} %bitcast.9, ...), custom_call_target="tpu_custom_call" | custom-call | tf_op jit(solution)/shard_map/pallas_call | solution.py:469
  56.1 2.6 %shard_map.93 = (bf16[512,1280]{1,0:T(8,128)(2,1)}, bf16[512,1280]{1,0:T(8,128)(2,1)}, f32[5,64]{1,0:T(8,128)}, bf16[1280,640]{1,0:T(8,128)(2,1)}, bf16[640,1280]{1,0:T(8,128)(2,1)}) custom-call(bf16[512,1280]{1,0:T(8,128)(2,1)S(1)} %get-tuple-element.15.a0, bf16[512,1280]{1,0:T(8,128)(2,1)S(1)} %get-tuple-element.16.a1, f32[5,64]{1,0:T(8,128)S(1)} %get-tuple-element.17.a2, ...), custom_call_target="tpu_custom_call" | custom-call | tf_op jit(solution)/shard_map/pallas_call | solution.py:511

commit v4 on v3

--- a/solution.py
+++ b/solution.py
@@ -14,7 +14,7 @@
 YS = 4
 XS = 4
 ZS = 8
-DIRECT = (0, 2)
+DIRECT = (0, 1, 2)
 NEAR = (1, 2, ZS - 2, ZS - 1)
 D = 1280
 H = 640
@@ -171,11 +171,8 @@
         all_of(ref, recv_sem.at[sem])
 
     def over_y(make):
-        def step(k, carry):
+        for k in (2, 1, 3):
             make(2 * lax.rem(y + k, YS) + core)
-            return carry
-
-        lax.fori_loop(1, YS, step, 0)
 
     def rs_core(i):
         send(rc[i].at[away], rm[i], 5 * i, twin, me_n)
@@ -208,15 +205,17 @@
         rows = jnp.concatenate(rows, axis=1)
         for k in range(XS):
             es[i][k] = rows[2 * k : 2 * k + 2].astype(es[i].dtype)
-        for k in range(XS):
-
-            @pl.when(ex_peer(k) != me_n)
-            def _():
-                send(es[i].at[k], er[i].at[x], 5 * i + 2, me_s, ex_peer(k))
-
-            @pl.when(ex_peer(k) == me_n)
-            def _():
-                er[i][x] = es[i][k]
+        for k in (2, 1, 3):
+            to = lax.rem(x + k, XS)
+            send(es[i].at[to], er[i].at[x], 5 * i + 2, me_s, ex_peer(to))
+
+        @pl.when(partner != z)
+        def _():
+            send(es[i].at[x], er[i].at[x], 5 * i + 2, me_s, ex_peer(x))
+
+        @pl.when(partner == z)
+        def _():
+            er[i][x] = es[i][x]
 
     def ex_rows(i):
         @pl.when(partner != z)
@@ -236,7 +235,7 @@
             piece = jnp.concatenate([piece, extra], axis=1)
         ag[i][4 * own + mine] = piece.astype(BF16)
         if i in DIRECT:
-            for k in range(1, SEQ):
+            for k in (4, 5, 3, 2, 6, 7, 1):
                 send(
                     ag[i].at[4 * own + mine], ag[i].at[4 * own + mine], 5 * i + 3, lax.rem(me_s + k, SEQ), me_n
                 )
@@ -387,12 +386,9 @@
                 ty_send[k, j, i] = tc_sum[k, pl.ds(5 * j + i, 4, stride=20), :]
     ty_recv[XS * y + x] = ty_send[y, x]
 
-    def send_yx(k, carry):
+    for k in (10, 9, 11, 6, 14, 8, 2, 5, 7, 13, 15, 4, 12, 1, 3):
         s, n = yx_peer(k)
         send(ty_send.at[s // 2, lax.rem(n, XS)], ty_recv.at[XS * y + x], 23, s, n)
-        return carry
-
-    lax.fori_loop(1, YS * XS, send_yx, 0)
     weights = jnp.concatenate([dispatch, d_logit], axis=0).T.astype(BF16)
     values = jnp.concatenate([d_slots, router_t], axis=0)
     for k in range(4):
@@ -411,12 +407,10 @@
                 tz_send[4 * half + i, k : k + 1] = packed[i : i + 1]
     tz_recv[z] = tz_send[z]
 
-    def send_z(k, carry):
+    for k in (4, 3, 5, 2, 6, 1, 7):
         to = lax.rem(z + k, ZS)
         send(tz_send.at[to], tz_recv.at[z], 24, me_s, XS * to + x)
-        return carry
-
-    lax.fori_loop(1, ZS, send_z, 0)
+
     arrived(tz_recv.at[pl.ds(0, ZS - 1)], 24)
     total = tz_recv[0]
     for k in range(1, ZS):

time: 59 us -> 56.4 us (0.956)
  Pallas kernels: 58.1 us -> 55.4 us
    pallas_call x1, Pallas kernels: 55.5 us -> 52.8 us  [shards(): pl.pallas_call(kernel, out_shape=(vmem((T, D), BF16), vmem((T, D), BF16),...]
where the time goes in v4:
time: 56.4 us; the launch traced here: 56.1 us
  Pallas kernels  55.4 us (98%)
  between operations  0.64 us (1%)
    pallas_call x1, Pallas kernels, shards(): pl.pallas_call(kernel, out_shape=(vmem((T, D), BF16), vmem((T, D), BF16),...  52.8 us
    pallas_call x1, Pallas kernels, shards(): pl.pallas_call(store, out_shape=tuple((jax.ShapeDtypeStruct(r.shape, r.dt...  2.62 us

profile of v4, /device:TPU:1, one launch (start us, length us, event | category | flops | bytes accessed | tf_op | source)
XLA Modules:
  0.0 56.1 jit_solution(4095220142418431326)
XLA Ops:
  0.6 52.8 %shard_map.92 = (bf16[512,1280]{1,0:T(8,128)(2,1)S(1)}, bf16[512,1280]{1,0:T(8,128)(2,1)S(1)}, f32[5,64]{1,0:T(8,128)S(1)}, bf16[1280,640]{1,0:T(8,128)(2,1)S(1)}, bf16[640,1280]{1,0:T(8,128)(2,1)S(1)}) custom-call(bf16[512,1280]{1,0:T(8,128)(2,1)} %bitcast.11, bf16[64,1280]{1,0:T(8,128)(2,1)} %bitcast.13, bf16[1280,640]{1,0:T(8,128)(2,1)} %bitcast.9, ...), custom_call_target="tpu_custom_call" | custom-call | tf_op jit(solution)/shard_map/pallas_call | solution.py:463
  53.4 2.6 %shard_map.93 = (bf16[512,1280]{1,0:T(8,128)(2,1)}, bf16[512,1280]{1,0:T(8,128)(2,1)}, f32[5,64]{1,0:T(8,128)}, bf16[1280,640]{1,0:T(8,128)(2,1)}, bf16[640,1280]{1,0:T(8,128)(2,1)}) custom-call(bf16[512,1280]{1,0:T(8,128)(2,1)S(1)} %get-tuple-element.15.a0, bf16[512,1280]{1,0:T(8,128)(2,1)S(1)} %get-tuple-element.16.a1, f32[5,64]{1,0:T(8,128)S(1)} %get-tuple-element.17.a2, ...), custom_call_target="tpu_custom_call" | custom-call | tf_op jit(solution)/shard_map/pallas_call | solution.py:505

commit v5 on v4

--- a/solution.py
+++ b/solution.py
@@ -97,14 +97,15 @@
     tokens_hbm, router_hbm, w_in_hbm, w_out_hbm, grad_hbm,
     mixed_v, d_tok_v, d_rout_v, d_w_in_v, d_w_out_v,
     tok, rout, w_in, w_out, grad,
-    rc0, rc1, rc2, rc3, rm0, rm1, rm2, rm3, ry0, ry1, ry2, ry3, rr0, rr1, rr2, rr3,
-    es0, es1, es2, es3, er0, er1, er2, er3, ag0, ag1, ag2, ag3,
+    rc0, rc1, rc2, rc3, rc4, rm0, rm1, rm2, rm3, rm4, ry0, ry1, ry2, ry3, ry4, rr0, rr1, rr2, rr3, rr4,
+    es0, es1, es2, es3, es4, er0, er1, er2, er3, er4, ag0, ag1, ag2, ag3,
     st_send, st_mid, st_core, st_recv, weight,
     tc_send, tc_mid, tc_sum, ty_send, ty_recv, tz_send, tz_recv,
     in_sem, send_sem, recv_sem, hello,
 ):
-    rc, rm, ry, rr = (rc0, rc1, rc2, rc3), (rm0, rm1, rm2, rm3), (ry0, ry1, ry2, ry3), (rr0, rr1, rr2, rr3)
-    es, er, ag = (es0, es1, es2, es3), (er0, er1, er2, er3), (ag0, ag1, ag2, ag3)
+    rc, rm = (rc0, rc1, rc2, rc3, rc4), (rm0, rm1, rm2, rm3, rm4)
+    ry, rr = (ry0, ry1, ry2, ry3, ry4), (rr0, rr1, rr2, rr3, rr4)
+    es, er, ag = (es0, es1, es2, es3, es4), (er0, er1, er2, er3, er4), (ag0, ag1, ag2, ag3)
     me_s = lax.axis_index("seq")
     me_n = lax.axis_index("exp")
     y = me_s // 2
@@ -267,38 +268,49 @@
     own_exp = jnp.exp(logits - own_top)
     st_send[...] = pair_rows(own_top, jnp.sum(own_exp, axis=1, keepdims=True))
     exp_high, exp_low = split(own_exp)
-    store_blocks(rc[1], nn(exp_high, tok[...]) + nn(exp_low, tok[...]))
+    in_part = nn(exp_high, tok[...]) + nn(exp_low, tok[...])
+    store_blocks(rc[1], in_part)
 
     pl.semaphore_wait(barrier, 1 + YS - 1 + XS - 1 + len(NEAR))
     rs_core(1)
-    send(st_send, st_mid, 20, twin, me_n)
+    send(st_send, st_mid, 25, twin, me_n)
     pass_on(0, along_x + along_z)
     row_exp = jnp.exp(logits - jnp.max(logits, axis=0, keepdims=True))
     combine = row_exp / jnp.sum(row_exp, axis=0, keepdims=True)
     loads[1].wait()
     store_blocks(rc[0], nn(combine.astype(BF16), grad[...]))
     rs_core(0)
-
-    arrived(st_mid, 20)
+    store_blocks(rc[4], split(in_part)[1])
+    rs_core(4)
+
+    arrived(st_mid, 25)
     top, total, (w_own, w_mid) = merge([st_send[...], st_mid[...]])
     st_core[...] = left(top, total)
     weight[...] = columns(left(w_own, w_mid))
+
+    def spread(w):
+        return jnp.concatenate([jnp.concatenate([w] * 5, axis=1)] * 2, axis=0)
+
+    def weighted(i, k):
+        g = pl.multiple_of(8 * (own + 2 * k), 8)
+        a, b = spread(weight[pl.ds(g, 8)]), spread(weight[pl.ds(S + g, 8)])
+        return rc[i][own, k].astype(F32) * a + rm[i][k].astype(F32) * b
+
     arrived(rm[1], 5)
     for k in range(YS):
-        g = pl.multiple_of(8 * (own + 2 * k), 8)
-        a = weight[pl.ds(g, 8)]
-        b = weight[pl.ds(S + g, 8)]
-        a = jnp.concatenate([jnp.concatenate([a] * 5, axis=1)] * 2, axis=0)
-        b = jnp.concatenate([jnp.concatenate([b] * 5, axis=1)] * 2, axis=0)
-        ry[1][k] = rc[1][own, k] * a + rm[1][k] * b
+        ry[1][k] = weighted(1, k).astype(BF16)
     st_recv[y] = st_core[...]
-    over_y(lambda s: send(st_core, st_recv.at[y], 21, s, me_n))
+    over_y(lambda s: send(st_core, st_recv.at[y], 26, s, me_n))
     rs_y_send(1)
     rs_y(0)
     pl.semaphore_wait(hello.at[0], XS - 1 + len(NEAR))
     pass_on(1, along_z)
-
-    arrived(st_recv.at[pl.ds(0, YS - 1)], 21)
+    arrived(rm[4], 20)
+    for k in range(YS):
+        ry[4][k] = (split(weighted(1, k))[1].astype(F32) + weighted(4, k)).astype(BF16)
+    rs_y_send(4)
+
+    arrived(st_recv.at[pl.ds(0, YS - 1)], 26)
     stats = [st_recv[k] for k in range(YS)]
     top, total, ws = merge(stats)
     w = [v / total for v in ws]
@@ -310,12 +322,17 @@
     arrived(rr[1].at[pl.ds(0, YS - 1)], 6)
     total_in = jnp.zeros((16, H), F32)
     for k, v in enumerate((w0, w1, w2, w3)):
-        total_in = total_in + rr[1][k] * jnp.concatenate([jnp.concatenate([v] * 5, axis=1)] * 2, axis=0)
+        total_in = total_in + rr[1][k].astype(F32) * spread(v)
     pl.semaphore_wait(hello.at[1], len(NEAR))
     ex_start(1, total_in)
     ex_start(0, rs_total(0))
     scale = columns(left(jnp.exp(st_send[...] - top) / total, total))[:S, :1]
     dispatch = own_exp * scale
+    arrived(rr[4].at[pl.ds(0, YS - 1)], 21)
+    total_low = split(total_in)[1].astype(F32)
+    for k, v in enumerate((w0, w1, w2, w3)):
+        total_low = total_low + rr[4][k].astype(F32) * spread(v)
+    ex_start(4, total_low)
 
     rows_1 = ex_rows(1)
     ag_start(1, rows_1)
@@ -346,6 +363,7 @@
         d_w_out_v[part] = nn(act_t[part], d_rows).astype(BF16)
     ex_start(3, rs_total(3))
     total = rs_total(2).astype(BF16).astype(F32)
+    rows_1 = rows_1 + ex_rows(4)
     column = jnp.sum(total[:8] * rows_1[:, :H] + total[8:] * rows_1[:, H:], axis=1, keepdims=True)
     ex_start(2, total, thirds(column))
     rows_t = rows.astype(F32).T.astype(BF16)
@@ -372,12 +390,12 @@
     pair = jnp.concatenate([d_router_t, pltpu.roll(d_router_t, D - 80, 1)], axis=0).T
     for k in range(SEQ):
         tc_send[k % 2, k // 2] = pair[160 * k : 160 * k + 80]
-    send(tc_send.at[1 - core], tc_mid, 22, twin, me_n)
+    send(tc_send.at[1 - core], tc_mid, 27, twin, me_n)
     combine_t = combine.T.astype(BF16)
     for k in range(4):
         part = slice(128 * k, 128 * k + 128)
         mixed_v[part] = nn(combine_t[part], slots_out).astype(BF16)
-    arrived(tc_mid, 22)
+    arrived(tc_mid, 27)
     for k in range(YS):
         tc_sum[k] = tc_send[core, k] + tc_mid[k]
     for k in range(YS):
@@ -388,13 +406,13 @@
 
     for k in (10, 9, 11, 6, 14, 8, 2, 5, 7, 13, 15, 4, 12, 1, 3):
         s, n = yx_peer(k)
-        send(ty_send.at[s // 2, lax.rem(n, XS)], ty_recv.at[XS * y + x], 23, s, n)
+        send(ty_send.at[s // 2, lax.rem(n, XS)], ty_recv.at[XS * y + x], 28, s, n)
     weights = jnp.concatenate([dispatch, d_logit], axis=0).T.astype(BF16)
     values = jnp.concatenate([d_slots, router_t], axis=0)
     for k in range(4):
         part = slice(128 * k, 128 * k + 128)
         d_tok_v[part] = nn(weights[part], values).astype(BF16)
-    arrived(ty_recv.at[pl.ds(0, YS * XS - 1)], 23)
+    arrived(ty_recv.at[pl.ds(0, YS * XS - 1)], 28)
     total = ty_recv[0]
     for k in range(1, YS * XS):
         total = total + ty_recv[k]
@@ -409,9 +427,9 @@
 
     for k in (4, 3, 5, 2, 6, 1, 7):
         to = lax.rem(z + k, ZS)
-        send(tz_send.at[to], tz_recv.at[z], 24, me_s, XS * to + x)
-
-    arrived(tz_recv.at[pl.ds(0, ZS - 1)], 24)
+        send(tz_send.at[to], tz_recv.at[z], 29, me_s, XS * to + x)
+
+    arrived(tz_recv.at[pl.ds(0, ZS - 1)], 29)
     total = tz_recv[0]
     for k in range(1, ZS):
         total = total + tz_recv[k]
@@ -419,7 +437,7 @@
     for k in range(5):
         d_rout_v[k : k + 1] = (other if k % 2 else total)[k // 2 : k // 2 + 1, :S]
 
-    for i in range(4):
+    for i in range(5):
         all_of(rm[i], send_sem.at[5 * i])
         all_of(rr[i].at[pl.ds(0, YS - 1)], send_sem.at[5 * i + 1])
 
@@ -431,16 +449,18 @@
         def _():
             all_of(er[i].at[pl.ds(0, XS - 1)], send_sem.at[5 * i + 2])
 
+        if i == 4:
+            continue
         if i in DIRECT:
             all_of(ag[i].at[pl.ds(0, SEQ - 1)], send_sem.at[5 * i + 3])
         else:
             all_of(ag[i].at[pl.ds(0, YS - 1)], send_sem.at[5 * i + 3])
             all_of(ag[i].at[pl.ds(0, YS)], send_sem.at[5 * i + 4])
-    all_of(st_mid, send_sem.at[20])
-    all_of(st_recv.at[pl.ds(0, YS - 1)], send_sem.at[21])
-    all_of(tc_mid, send_sem.at[22])
-    all_of(ty_recv.at[pl.ds(0, YS * XS - 1)], send_sem.at[23])
-    all_of(tz_recv.at[pl.ds(0, ZS - 1)], send_sem.at[24])
+    all_of(st_mid, send_sem.at[25])
+    all_of(st_recv.at[pl.ds(0, YS - 1)], send_sem.at[26])
+    all_of(tc_mid, send_sem.at[27])
+    all_of(ty_recv.at[pl.ds(0, YS * XS - 1)], send_sem.at[28])
+    all_of(tz_recv.at[pl.ds(0, ZS - 1)], send_sem.at[29])
 
 
 def store(a0, a1, a2, a3, a4, b0, b1, b2, b3, b4, sem):
@@ -458,8 +478,8 @@
     any_space = pl.BlockSpec(memory_space=pl.ANY)
     dma = pltpu.SemaphoreType.DMA
     vmem = pltpu.VMEM
-    kinds = (BF16, F32, BF16, BF16)
     wide = (0, 0, 128, 0)
+    rest = (0,)
     results = pl.pallas_call(
         kernel,
         out_shape=(
@@ -477,12 +497,12 @@
             vmem((D, H), BF16),
             vmem((H, D), BF16),
             vmem((T, D), BF16),
-            *[vmem((2, 4, 16, H), k) for k in kinds],
-            *[vmem((4, 16, H), k) for k in kinds],
-            *[vmem((4, 16, H), k) for k in kinds],
-            *[vmem((4, 16, H), k) for k in kinds],
-            *[vmem((XS, 2, D + w), k) for w, k in zip(wide, kinds)],
-            *[vmem((XS, 2, D + w), k) for w, k in zip(wide, kinds)],
+            *[vmem((2, 4, 16, H), BF16) for _ in wide + rest],
+            *[vmem((4, 16, H), BF16) for _ in wide + rest],
+            *[vmem((4, 16, H), BF16) for _ in wide + rest],
+            *[vmem((4, 16, H), BF16) for _ in wide + rest],
+            *[vmem((XS, 2, D + w), BF16) for w in wide + rest],
+            *[vmem((XS, 2, D + w), BF16) for w in wide + rest],
             *[vmem((SEQ, 16, H + w), BF16) for w in wide],
             vmem((8, 128), F32),
             vmem((8, 128), F32),
@@ -496,7 +516,7 @@
             vmem((YS * XS, 5, 4, 128), F32),
             vmem((ZS, 4, 128), F32),
             vmem((ZS, 4, 128), F32),
-            dma((8,)), dma((25,)), dma((25,)), pltpu.SemaphoreType.REGULAR((2,)),
+            dma((8,)), dma((30,)), dma((30,)), pltpu.SemaphoreType.REGULAR((2,)),
         ],
         compiler_params=pltpu.CompilerParams(
             collective_id=0, has_side_effects=True, vmem_limit_bytes=VMEM

time: 56.4 us -> 55.8 us (0.989)
  Pallas kernels: 55.4 us -> 54.8 us
    pallas_call x1, Pallas kernels: 52.8 us -> 52.2 us  [shards(): pl.pallas_call(kernel, out_shape=(vmem((T, D), BF16), vmem((T, D), BF16),...]
where the time goes in v5:
time: 55.8 us; the launch traced here: 55.5 us
  Pallas kernels  54.8 us (98%)
  between operations  0.64 us (1%)
    pallas_call x1, Pallas kernels, shards(): pl.pallas_call(kernel, out_shape=(vmem((T, D), BF16), vmem((T, D), BF16),...  52.2 us
    pallas_call x1, Pallas kernels, shards(): pl.pallas_call(store, out_shape=tuple((jax.ShapeDtypeStruct(r.shape, r.dt...  2.62 us

profile of v5, /device:TPU:1, one launch (start us, length us, event | category | flops | bytes accessed | tf_op | source)
XLA Modules:
  0.0 55.5 jit_solution(12308471898313618492)
XLA Ops:
  0.6 52.2 %shard_map.92 = (bf16[512,1280]{1,0:T(8,128)(2,1)S(1)}, bf16[512,1280]{1,0:T(8,128)(2,1)S(1)}, f32[5,64]{1,0:T(8,128)S(1)}, bf16[1280,640]{1,0:T(8,128)(2,1)S(1)}, bf16[640,1280]{1,0:T(8,128)(2,1)S(1)}) custom-call(bf16[512,1280]{1,0:T(8,128)(2,1)} %bitcast.11, bf16[64,1280]{1,0:T(8,128)(2,1)} %bitcast.13, bf16[1280,640]{1,0:T(8,128)(2,1)} %bitcast.9, ...), custom_call_target="tpu_custom_call" | custom-call | tf_op jit(solution)/shard_map/pallas_call | solution.py:483
  52.9 2.6 %shard_map.93 = (bf16[512,1280]{1,0:T(8,128)(2,1)}, bf16[512,1280]{1,0:T(8,128)(2,1)}, f32[5,64]{1,0:T(8,128)}, bf16[1280,640]{1,0:T(8,128)(2,1)}, bf16[640,1280]{1,0:T(8,128)(2,1)}) custom-call(bf16[512,1280]{1,0:T(8,128)(2,1)S(1)} %get-tuple-element.15.a0, bf16[512,1280]{1,0:T(8,128)(2,1)S(1)} %get-tuple-element.16.a1, f32[5,64]{1,0:T(8,128)S(1)} %get-tuple-element.17.a2, ...), custom_call_target="tpu_custom_call" | custom-call | tf_op jit(solution)/shard_map/pallas_call | solution.py:525

commit v6 on v5

--- a/solution.py
+++ b/solution.py
@@ -280,8 +280,6 @@
     loads[1].wait()
     store_blocks(rc[0], nn(combine.astype(BF16), grad[...]))
     rs_core(0)
-    store_blocks(rc[4], split(in_part)[1])
-    rs_core(4)
 
     arrived(st_mid, 25)
     top, total, (w_own, w_mid) = merge([st_send[...], st_mid[...]])
@@ -303,6 +301,8 @@
     over_y(lambda s: send(st_core, st_recv.at[y], 26, s, me_n))
     rs_y_send(1)
     rs_y(0)
+    store_blocks(rc[4], split(in_part)[1])
+    rs_core(4)
     pl.semaphore_wait(hello.at[0], XS - 1 + len(NEAR))
     pass_on(1, along_z)
     arrived(rm[4], 20)

time: 55.8 us -> 55.8 us (level)
  no operation moved by 1% of the time
where the time goes in v6:
time: 55.8 us; the launch traced here: 55.1 us
  Pallas kernels  54.4 us (97%)
  between operations  0.64 us (1%)
    pallas_call x1, Pallas kernels, shards(): pl.pallas_call(kernel, out_shape=(vmem((T, D), BF16), vmem((T, D), BF16),...  51.8 us
    pallas_call x1, Pallas kernels, shards(): pl.pallas_call(store, out_shape=tuple((jax.ShapeDtypeStruct(r.shape, r.dt...  2.62 us

profile of v6, /device:TPU:1, one launch (start us, length us, event | category | flops | bytes accessed | tf_op | source)
XLA Modules:
  0.0 55.1 jit_solution(15127616343443673931)
XLA Ops:
  0.6 51.8 %shard_map.92 = (bf16[512,1280]{1,0:T(8,128)(2,1)S(1)}, bf16[512,1280]{1,0:T(8,128)(2,1)S(1)}, f32[5,64]{1,0:T(8,128)S(1)}, bf16[1280,640]{1,0:T(8,128)(2,1)S(1)}, bf16[640,1280]{1,0:T(8,128)(2,1)S(1)}) custom-call(bf16[512,1280]{1,0:T(8,128)(2,1)} %bitcast.11, bf16[64,1280]{1,0:T(8,128)(2,1)} %bitcast.13, bf16[1280,640]{1,0:T(8,128)(2,1)} %bitcast.9, ...), custom_call_target="tpu_custom_call" | custom-call | tf_op jit(solution)/shard_map/pallas_call | solution.py:483
  52.4 2.6 %shard_map.93 = (bf16[512,1280]{1,0:T(8,128)(2,1)}, bf16[512,1280]{1,0:T(8,128)(2,1)}, f32[5,64]{1,0:T(8,128)}, bf16[1280,640]{1,0:T(8,128)(2,1)}, bf16[640,1280]{1,0:T(8,128)(2,1)}) custom-call(bf16[512,1280]{1,0:T(8,128)(2,1)S(1)} %get-tuple-element.15.a0, bf16[512,1280]{1,0:T(8,128)(2,1)S(1)} %get-tuple-element.16.a1, f32[5,64]{1,0:T(8,128)S(1)} %get-tuple-element.17.a2, ...), custom_call_target="tpu_custom_call" | custom-call | tf_op jit(solution)/shard_map/pallas_call | solution.py:525
